TPU v7x, 32 devices: a whole 2x2x4 slice. The times are simulated.
32 devices in a mesh: groups: 2 (over x), req: 16 (over z, y, core).
Axes of the slice: x: 2, y: 2, z: 4, core: 2. Of those that a mesh axis runs over, the one named last changes fastest.
Arguments:
- saved_hidden: bfloat16 [2048, 8, 8192], P(('groups', 'req')), parts along dimension 0, may hold values from -6 to 6
- kv_weight: bfloat16 [8192, 1024], replicated, may hold values from -0.0625 to 0.0625
- queries: bfloat16 [128, 4096], P(('groups', 'req')), parts along dimension 0, may hold values from -30 to 30
- new_kv: bfloat16 [128, 1024], P(('groups', 'req')), parts along dimension 0, may hold values from -3 to 3
- hist_blocks: int32 [8], P('groups'), parts along dimension 0, may hold values from 1 to 256, 512 in all
- new_len: int32 [8], P('groups'), parts along dimension 0, may hold values from 1 to 16, 48 in all
- pack_order: int32 [8], P('groups'), parts along dimension 0, may hold values from 0 to 3, each once
- holder_slot: int32 [1024], P('groups'), parts along dimension 0, may hold values from 0 to 1023, as said below
Outputs:
- restored_cache: bfloat16 [1024, 8, 1024], P(('groups', 'req')), parts along dimension 0
- attention: bfloat16 [128, 4096], P(('groups', 'req')), parts along dimension 0
There are 2 independent parts, one for each index of `groups`. A program takes and returns all parts, laid end to end along the dimension named above; an argument that names none is the same for every part. Nothing has to cross between parts.
Inputs may be any that keep to these rules, and one draw needn't show every extreme that they name: `hist_blocks`: their sum is 512. `new_len`: their sum is three quarters of 64, rounded down. `pack_order`: A permutation of the requests. Device holder_slot // 64 of req keeps block g's saved rows at its local slot holder_slot % 64; no slot holds two blocks. Exactly half of the devices of req hold saved blocks, the first and the last device among them, each 64 blocks; of the 32 blocks n * 32 to (n + 1) * 32 - 1, each such device holds exactly 4, for every n.
All inputs are finite; a program needn't handle non-finite values.
Results may differ from a plain program's by a relative error of at most 0.01.
The roundings to bfloat16 on the way count: a program that leaves them out, or rounds other values in their place, can miss the bound.
Values may be sent and summed in bfloat16 or wider, within the bound.
No kernel may reach another device: no remote copies, remote signals or barrier semaphores. Data moves between devices by JAX's collectives and lax.ppermute only.
A program may use at most 128 MiB of HBM per device.

v0:
```python
import jax
import jax.numpy as jnp
from jax import lax
from jax.sharding import PartitionSpec as P

KVH = 4
QPK = 8
HD = 128
NEWT = 16


rope_base = 500000.0
masked_score = -1e30


def rotate(values, positions):
    half_width = HD // 2
    frequency = rope_base ** (-(jnp.arange(half_width, dtype=jnp.float32) * 2.0 / HD))
    angles = positions.astype(jnp.float32)[..., None] * frequency
    cosine = jnp.cos(angles)
    sine_part = jnp.sin(angles)
    first_half = values[..., :half_width]
    second_half = values[..., half_width:]
    return jnp.concatenate(
        [
            first_half * cosine - second_half * sine_part,
            second_half * cosine + first_half * sine_part,
        ],
        axis=-1,
    )


def layout(hist_blocks, pack_order):
    request_ids = jnp.arange(hist_blocks.shape[0], dtype=jnp.int32)
    onehot = (pack_order[:, None] == request_ids[None, :]).astype(jnp.int32)
    ordered = jnp.sum(onehot * hist_blocks[None, :], axis=1)
    ordered_start = jnp.cumsum(ordered) - ordered
    request_start = jnp.sum(onehot * ordered_start[:, None], axis=0)
    request_place = jnp.sum(onehot * request_ids[:, None], axis=0)
    return (request_start, request_place)


def slot_tables(request_start, hist_blocks, slot_ids):
    block_end = request_start + hist_blocks
    inside = (
        (slot_ids[:, None] >= request_start[None, :]) & (slot_ids[:, None] < block_end[None, :])
    ).astype(jnp.int32)
    request_ids = jnp.arange(hist_blocks.shape[0], dtype=jnp.int32)
    slot_request = jnp.sum(inside * request_ids[None, :], axis=1)
    slot_block = slot_ids - jnp.sum(inside * request_start[None, :], axis=1)
    return (slot_request, slot_block)


def finish(projected, positions):
    key_width = KVH * HD
    lead_shape = projected.shape[:-1]
    rotated = rotate(
        projected[..., :key_width].reshape(lead_shape + (KVH, HD)), positions[..., None]
    )
    rotated = rotated.reshape(lead_shape + (key_width,))
    return jnp.concatenate([rotated, projected[..., key_width:]], axis=-1).astype(jnp.bfloat16)


def partial_softmax(query_rot, key_rows, allowed):
    key_count = key_rows.shape[0]
    key_width = KVH * HD
    key_part = key_rows[:, :key_width].reshape(key_count, KVH, HD)
    value_part = key_rows[:, key_width:].reshape(key_count, KVH, HD)
    scores = jnp.einsum(
        "tgjd,sgd->gjts", query_rot, key_part, preferred_element_type=jnp.float32
    ) * HD ** (-0.5)
    scores = jnp.where(allowed[None, None], scores, masked_score)
    peak = jnp.max(scores, axis=-1)
    weights = jnp.exp(scores - peak[..., None])
    denominator = jnp.sum(weights, axis=-1)
    numerator = jnp.einsum(
        "gjts,sgd->tgjd",
        weights.astype(jnp.bfloat16),
        value_part,
        preferred_element_type=jnp.float32,
    )
    tokens = query_rot.shape[0]
    head_count = KVH * QPK
    return (
        jnp.transpose(peak, (2, 0, 1)).reshape(tokens, head_count),
        jnp.transpose(denominator, (2, 0, 1)).reshape(tokens, head_count),
        numerator.reshape(tokens, head_count, HD),
    )


def on_device(
    saved_hidden, kv_weight, queries, new_kv, hist_blocks, new_len, pack_order, holder_slot
):
    device_count = lax.axis_size("req")
    device = lax.axis_index("req")
    hold_slots, block_rows, model_width = saved_hidden.shape
    slot_count = holder_slot.shape[0]
    owned_blocks = slot_count // device_count
    capacity = hold_slots // device_count
    pair_width = kv_weight.shape[1]
    request_count = hist_blocks.shape[0]
    request_start, request_place = layout(hist_blocks, pack_order)
    slot_request, slot_block = slot_tables(
        request_start, hist_blocks, jnp.arange(slot_count, dtype=jnp.int32)
    )
    holder_device = holder_slot // hold_slots
    holders = holder_device.reshape(device_count, owned_blocks)
    storage = (holder_slot % hold_slots).reshape(device_count, owned_blocks)
    held_here = (holders == device).astype(jnp.int32)
    earlier_held = jnp.cumsum(held_here, axis=1) - held_here
    chosen = held_here[:, :, None] * (
        earlier_held[:, :, None] == jnp.arange(capacity, dtype=jnp.int32)[None, None, :]
    ).astype(jnp.int32)
    send_slot = jnp.sum(chosen * storage[:, :, None], axis=1).reshape(-1)
    send_live = jnp.sum(chosen, axis=1).reshape(-1)
    send_block = jnp.sum(
        chosen * slot_block.reshape(device_count, owned_blocks)[:, :, None], axis=1
    ).reshape(-1)
    my_holders = lax.dynamic_slice_in_dim(holder_device, device * owned_blocks, owned_blocks)
    my_requests = lax.dynamic_slice_in_dim(slot_request, device * owned_blocks, owned_blocks)
    same_holder = my_holders[:, None] == my_holders[None, :]
    local_ids = jnp.arange(owned_blocks, dtype=jnp.int32)
    earlier = local_ids[None, :] < local_ids[:, None]
    arrival = my_holders * capacity + jnp.sum((same_holder & earlier).astype(jnp.int32), axis=1)
    row_ids = jnp.arange(block_rows, dtype=jnp.int32)
    outgoing = saved_hidden[send_slot]
    outgoing = jnp.where(send_live[:, None, None] > 0, outgoing, jnp.zeros((), jnp.bfloat16))
    projected = jnp.einsum("ibd,dc->ibc", outgoing, kv_weight, preferred_element_type=jnp.float32)
    positions = send_block[:, None] * block_rows + row_ids[None, :]
    finished = finish(projected, positions).reshape(device_count, capacity, block_rows, pair_width)
    returned = lax.all_to_all(finished, "req", split_axis=0, concat_axis=0, tiled=True)
    restored = returned.reshape(device_count * capacity, block_rows, pair_width)[arrival]
    query_all, new_all = (
        lax.all_gather(queries, "req", axis=0, tiled=True),
        lax.all_gather(new_kv, "req", axis=0, tiled=True),
    )
    local_keys = restored.reshape(owned_blocks * block_rows, pair_width)
    key_request = jnp.repeat(my_requests, block_rows)
    offsets = jnp.arange(NEWT, dtype=jnp.int32)
    token_total = query_all.shape[0]
    head_count = KVH * QPK
    first_place = request_place[my_requests[0]]
    last_place = request_place[my_requests[owned_blocks - 1]]
    initial = (
        jnp.full((token_total, head_count), masked_score, jnp.float32),
        jnp.zeros((token_total, head_count), jnp.float32),
        jnp.zeros((token_total, head_count, HD), jnp.float32),
    )

    def visit(position, carry):
        request = pack_order[position]
        history = hist_blocks[request]
        live_new = new_len[request]
        at_home = request_start[request] // owned_blocks == device
        new_positions = history * block_rows + offsets
        query_rows = (
            lax.dynamic_slice_in_dim(query_all, request * NEWT, NEWT, 0)
            .astype(jnp.float32)
            .reshape(NEWT, KVH, QPK, HD)
        )
        query_rot = rotate(query_rows, new_positions[:, None, None]).astype(jnp.bfloat16)
        new_rows = finish(
            lax.dynamic_slice_in_dim(new_all, request * NEWT, NEWT, 0).astype(jnp.float32),
            new_positions,
        )
        key_rows = jnp.concatenate([local_keys, new_rows], axis=0)
        hist_ok = key_request == request
        new_ok = (offsets[None, :] <= offsets[:, None]) & (offsets[None, :] < live_new) & at_home
        allowed = jnp.concatenate(
            [jnp.broadcast_to(hist_ok[None, :], (NEWT, hist_ok.shape[0])), new_ok], axis=1
        )
        pieces = partial_softmax(query_rot, key_rows, allowed)
        return tuple(
            (
                lax.dynamic_update_slice_in_dim(stacked, update, request * NEWT, 0)
                for stacked, update in zip(carry, pieces)
            )
        )

    peaks, totals, numerators = lax.fori_loop(first_place, last_place + 1, visit, initial)
    rows_local = queries.shape[0]
    global_peak = lax.pmax(peaks, "req")
    factor = jnp.exp(peaks - global_peak)
    totals_mine, numerators_mine = (
        lax.psum_scatter(
            (totals * factor).astype(jnp.bfloat16), "req", scatter_dimension=0, tiled=True
        ).astype(jnp.float32),
        lax.psum_scatter(
            (numerators * factor[..., None]).astype(jnp.bfloat16),
            "req",
            scatter_dimension=0,
            tiled=True,
        ).astype(jnp.float32),
    )
    global_rows = device * rows_local + jnp.arange(rows_local, dtype=jnp.int32)
    row_request = global_rows // NEWT
    row_offset = global_rows % NEWT
    row_limit = jnp.sum(
        (row_request[:, None] == jnp.arange(request_count, dtype=jnp.int32)[None, :]).astype(
            jnp.int32
        )
        * new_len[None, :],
        axis=1,
    )
    attention = numerators_mine / totals_mine[..., None]
    attention = jnp.where((row_offset < row_limit)[:, None, None], attention, 0.0)
    return (restored, attention.reshape(rows_local, head_count * HD).astype(jnp.bfloat16))


def solution(mesh):
    return jax.shard_map(
        on_device,
        mesh=mesh,
        in_specs=(
            P(("groups", "req"), None, None),
            P(),
            P(("groups", "req"), None),
            P(("groups", "req"), None),
            P("groups"),
            P("groups"),
            P("groups"),
            P("groups"),
        ),
        out_specs=(P(("groups", "req"), None, None), P(("groups", "req"), None)),
        check_vma=False,
    )
```

profile of v0, /device:TPU:0, one launch (start us, length us, event | category | flops | bytes accessed | tf_op | source)
XLA Modules:
  0.0 262.6 jit_solution(14983668904531531246)
XLA Ops:
  7.2 0.7 add_select_fusion
  7.9 0.7 compare_convert_fusion
  8.8 0.9 select_reduce_fusion.6
  9.9 0.7 select_reduce_fusion.3
  10.6 0.7 add.185
  12.3 8.9 %gather_fusion = bf16[64,8,8192]{2,1,0:T(8,128)(2,1)} fusion(bf16[64,8,8192]{2,1,0:T(8,128)(2,1)} %param.10, s32[1024]{0:T(1024)S(1)} %pad_clamp_fusion.1), kind=kCustom, calls=%fused_computation | custom fusion | bytes 16777472 | tf_op jit(solution)/shard_map/gather | solution.py:126
  21.2 14.4 %fusion.20 = f32[64,8,1024]{2,1,0:T(8,128)S(1)} fusion(bf16[8192,1024]{1,0:T(8,128)(2,1)} %param.11, bf16[64,8,8192]{2,1,0:T(8,128)(2,1)} %gather_fusion, pred[64]{0:T(512)(128)(4,1)S(1)} %gt.16), kind=kOutput, calls=%fused_computation.39 | convolution fusion | flops 8594128896 | bytes 27263040 | tf_op jit(solution)/shard_map/ibd,dc->ibc/dot_general | solution.py:128
  36.1 1.0 multiply_cosine_fusion.1
  37.1 0.5 subtract_convert_fusion.2
  38.0 1.1 pad_maximum_fusion.1
  39.1 7.4 %all-to-all-start = ((bf16[16,4,8,1024]{3,2,1,0:T(8,128)(2,1)}), bf16[16,4,8,1024]{3,2,1,0:T(8,128)(2,1)S(1)}, u32[]{:S(2)}, u32[]{:S(2)}) async-start(bf16[16,4,8,1024]{3,2,1,0:T(8,128)(2,1)} %pad_maximum_fusion.1), calls=%async_computation | async-start | bytes 2097152 | tf_op jit(solution)/shard_map/all_to_all | solution.py:131
  46.6 0.7 fusion.38
  49.8 31.9 %all-gather.1 = bf16[16,4,4096]{2,1,0:T(4,128)(2,1)S(1)} all-gather(bf16[1,4,4096]{2,1,0:T(4,128)(2,1)S(1)} %bitcast.94), channel_id=1, replica_groups=mesh['groups'=2,'req'=16] {'req'}, dimensions={0}, use_global_device_ids=true | all-gather | bytes 557056 | tf_op jit(solution)/shard_map/all_gather | solution.py:134
  81.7 0.9 reshape.501
  82.6 21.9 %all-gather = bf16[16,4,1024]{2,1,0:T(4,128)(2,1)S(1)} all-gather(bf16[1,4,1024]{2,1,0:T(4,128)(2,1)S(1)} %bitcast.96), channel_id=1, replica_groups=mesh['groups'=2,'req'=16] {'req'}, dimensions={0}, use_global_device_ids=true | all-gather | bytes 139264 | tf_op jit(solution)/shard_map/all_gather | solution.py:135
  105.8 0.6 fusion.37
  107.4 0.6 gather_fusion.1
  108.1 17.1 %while.19 = (s32[]{:T(128)}, f32[64,32]{0,1:T(8,128)S(1)}, f32[64,32]{0,1:T(8,128)S(1)}, f32[64,32,128]{2,1,0:T(8,128)S(1)}, s32[]{:T(128)}, /*index=5*/s32[4]{0...) while((s32[]{:T(128)}, f32[64,32]{0,1:T(8,128)S(1)}, ...), condition=%wide.region_15.16_spmd.clone.clone, body=%wide.region_12.15_spmd.clone.clone.sunk | while | flops 74618320 | bytes 8641948 | solution.py:180
  110.4 0.7 dynamic_slice.80
  113.9 0.6 dynamic_slice.81
  115.5 0.9 convert_bitcast_fusion.2
  117.0 0.6 dynamic_slice.82
  119.8 0.6 dynamic_slice.83
  120.4 0.6 iota_compare_fusion.9
  121.2 0.7 broadcast_compare_fusion.4
  125.3 74.7 %pmax.7 = f32[64,32]{0,1:T(8,128)S(1)} all-reduce(f32[64,32]{0,1:T(8,128)S(1)} %get-tuple-element.242), channel_id=1, replica_groups=mesh['groups'=2,'req'=16] {'req'}, use_global_device_ids=true, to_apply=%region_16.17 | all-reduce | flops 2048 | bytes 16384 | tf_op jit(solution)/shard_map/pmax | solution.py:182
  200.0 1.1 multiply_convert_fusion
  201.2 0.6 dynamic-slice
  202.7 30.1 %all-reduce = bf16[64,32]{0,1:T(8,128)(2,1)S(1)} all-reduce(bf16[64,32]{0,1:T(8,128)(2,1)S(1)} %get-tuple-element.348), channel_id=3, replica_groups=mesh['groups'=2,'req'=16] {'req'}, use_global_device_ids=true, to_apply=%region_18.19.clone | all-reduce | flops 2048 | bytes 8192
  233.0 21.3 %reduce-scatter.3.cloned.1.call-done = bf16[4,32,128]{2,1,0:T(8,128)(2,1)} async-done(((bf16[64,32,128]{2,1,0:T(8,128)(2,1)}), bf16[4,32,128]{2,1,0:T(8,128)(2,1)}) %reduce-scatter.3.cloned.1.call-update) | async-done | bytes 32784 | tf_op jit(solution)/shard_map/reduce_scatter | solution.py:188
  254.3 0.8 fusion.27
  255.1 0.6 copy.76
  (85 shorter events, 6.1 us)
Async XLA Ops:
  35.6 14.2 %copy-start.1 = (bf16[4,4096]{1,0:T(4,128)(2,1)S(1)}, bf16[4,4096]{1,0:T(4,128)(2,1)}, u32[]{:S(2)}) copy-start(bf16[4,4096]{1,0:T(4,128)(2,1)} %param.12) | copy-start | bytes 98308
  35.6 47.0 %copy-start.2 = (bf16[4,1024]{1,0:T(4,128)(2,1)S(1)}, bf16[4,1024]{1,0:T(4,128)(2,1)}, u32[]{:S(2)}) copy-start(bf16[4,1024]{1,0:T(4,128)(2,1)} %param.13) | copy-start | bytes 24580
  35.6 72.5 %copy-start.3 = (s32[4]{0:T(128)S(1)}, s32[4]{0:T(128)}, u32[]{:S(2)}) copy-start(s32[4]{0:T(128)} %param.16) | copy-start | bytes 52
  35.6 72.5 %copy-start.4 = (s32[4]{0:T(128)S(1)}, s32[4]{0:T(128)}, u32[]{:S(2)}) copy-start(s32[4]{0:T(128)} %param.14) | copy-start | bytes 52
  35.7 72.5 %copy-start.5 = (s32[4]{0:T(128)S(1)}, s32[4]{0:T(128)}, u32[]{:S(2)}) copy-start(s32[4]{0:T(128)} %param.15) | copy-start | bytes 52
  39.1 68.3 %all-to-all-start = ((bf16[16,4,8,1024]{3,2,1,0:T(8,128)(2,1)}), bf16[16,4,8,1024]{3,2,1,0:T(8,128)(2,1)S(1)}, u32[]{:S(2)}, u32[]{:S(2)}) async-start(bf16[16,4,8,1024]{3,2,1,0:T(8,128)(2,1)} %pad_maximum_fusion.1), calls=%async_computation | async-start | bytes 2097152 | tf_op jit(solution)/shard_map/all_to_all | solution.py:131
  46.5 207.8 %reduce-scatter.3.cloned.1.call-start = ((), (), s32[]{:S(2)}) async-start(), calls=%async_computation.2 | async-start | bytes 557056 | tf_op jit(solution)/shard_map/reduce_scatter | solution.py:188
  108.1 93.1 %copy-start.6 = (u32[32]{0:T(128)S(1)}, u32[32]{0:T(128)}, u32[]{:S(2)}) copy-start(u32[32]{0:T(128)} %constant.212) | copy-start | bytes 388
  125.3 130.5 %copy-start = (bf16[256,1024]{1,0:T(8,128)(2,1)}, bf16[256,1024]{1,0:T(8,128)(2,1)S(1)}, u32[]{:S(2)}) copy-start(bf16[256,1024]{1,0:T(8,128)(2,1)S(1)} %get-tuple-element.564) | copy-start | bytes 1572868
Sparse Core Ops, SparseCore 0:
  201.3 52.9 reduce-scatter.2
where the time goes:
time: 261 us; the launch traced here: 263 us
  blocking collectives  159 us (61%)
  waiting for transfers between devices  21.3 us (8%)
  between operations  19.4 us (7%)
  local copies, waits for them, and re-layouts  18 us (7%)
  matrix products  15.1 us (6%)
  other arithmetic  13.1 us (5%)
  loops' own time  9.65 us (4%)
  starting transfers between devices  7.42 us (3%)
    pmax x1, blocking collectives, on_device(): global_peak = lax.pmax(peaks, 'req')  74.7 us
    all_gather x1, blocking collectives, on_device(): lax.all_gather(queries, 'req', axis=0, tiled=True)  31.9 us
    unnamed x1, blocking collectives  30.1 us
    all_gather x1, blocking collectives, on_device(): lax.all_gather(new_kv, 'req', axis=0, tiled=True)  21.9 us
    reduce_scatter x1, waiting for transfers between devices, on_device(): lax.psum_scatter((numerators * factor[..., None]).astype(jnp.bfloat16), '...  21.3 us
    dot_general x1, matrix products, on_device(): jnp.einsum('ibd,dc->ibc', outgoing, kv_weight, preferred_element_type=jnp...  14.4 us
    another operation x1, loops' own time, on_device(): lax.fori_loop(first_place, last_place + 1, visit, initial)  9.65 us
    gather x1, local copies, waits for them, and re-layouts, on_device(): outgoing = saved_hidden[send_slot]  8.92 us
  transfers between devices with their start and end apart: 2, of which 1 were waited for; matrix products, arithmetic and copies ran while one was open for 1% of the time, Pallas kernels for 0%

commit v1 on v0

v1 whole, which is shorter than its diff:
```python
import functools

import jax
import jax.numpy as jnp
import numpy as np
from jax import lax
from jax.experimental import pallas as pl
from jax.experimental.pallas import tpu as pltpu
from jax.sharding import PartitionSpec as P

KVH = 4
QPK = 8
HD = 128
NEWT = 16
ROPE_BASE = 500000.0
MASKED = -1e30
SCALE = HD ** -0.5
F32 = jnp.float32
BF16 = jnp.bfloat16
I32 = jnp.int32
HALF = KVH * HD
LAYER = 4
ATTEND_WORK = 60 * 10**9
VM = pltpu.VMEM
SM = pltpu.SMEM
ANY = pl.ANY
HBM = pltpu.HBM


def frequencies():
    wave = ROPE_BASE ** (-(np.arange(HD // 2, dtype=np.float64) * 2.0 / HD))
    return np.concatenate([wave, wave]).astype(np.float32)[None, :]


def lane_sign(shape):
    lanes = lax.broadcasted_iota(I32, shape, len(shape) - 1)
    return jnp.where(lanes < HD // 2, -1.0, 1.0).astype(F32)


def specs(*spaces):
    return [pl.BlockSpec(memory_space=space) for space in spaces]


def call(kernel, name, inputs, spaces, outputs, out_spaces, scratch=(), mib=16, work=0):
    return pl.pallas_call(
        kernel,
        out_shape=tuple(jax.ShapeDtypeStruct(shape, kind) for shape, kind in outputs),
        in_specs=specs(*spaces),
        out_specs=tuple(specs(*out_spaces)),
        scratch_shapes=list(scratch),
        compiler_params=pltpu.CompilerParams(vmem_limit_bytes=mib << 20),
        cost_estimate=pl.CostEstimate(flops=work, transcendentals=0, bytes_accessed=0) if work else None,
        name=name,
    )(*inputs)


def split_sizes(width):
    return tuple(width // 16 * units for units in (1, 2, 3, 3, 3, 2, 2))


def iota(shape, axis):
    return lax.broadcasted_iota(I32, shape, axis)


def lane_total(values):
    return jnp.sum(values, axis=1, keepdims=True)


def spans(hist_ref, pack_ref):
    start = jnp.int32(0)
    for position in range(hist_ref.shape[0]):
        which = pack_ref[position]
        stop = start + hist_ref[which]
        yield which, start, stop
        start = stop


def places(device, holder, hist_ref, pack_ref, hold, owned, capacity):
    total = holder.shape[1]
    local = holder - device * hold
    held = (local >= 0) & (local < hold)
    blocks = iota((hold, total), 1)
    here = local == iota((hold, total), 0)
    block = lane_total(jnp.where(here, blocks, 0).astype(F32)).astype(I32)
    owner = block // owned
    rank = lane_total(jnp.where(held & (blocks < block) & (blocks >= owner * owned), 1.0, 0.0)).astype(I32)
    target = jnp.minimum(owner * capacity + jnp.minimum(rank, capacity - 1), hold - 1)
    target = jnp.where(lane_total(jnp.where(here, 1.0, 0.0)) > 0, target, iota((hold, 1), 0))
    depth = jnp.zeros((hold, 1), I32)
    for _, start, stop in spans(hist_ref, pack_ref):
        depth = jnp.where((block >= start) & (block < stop), block - start, depth)
    mine = device * owned
    blocks = iota((owned, total), 1)
    rows = iota((owned, total), 0) + mine
    keeper = holder // hold
    kept = lane_total(jnp.where(blocks == rows, keeper, 0).astype(F32)).astype(I32)
    order = lane_total(jnp.where((keeper == kept) & (blocks >= mine) & (blocks < rows), 1.0, 0.0)).astype(I32)
    arrival = kept * capacity + jnp.minimum(order, capacity - 1)
    arrival = jnp.concatenate([arrival, jnp.zeros((hold - owned, 1), I32)], axis=0)
    diagonal = iota((hold, HD), 0) == iota((hold, HD), 1)
    rows = [jnp.sum(jnp.where(diagonal, column, 0).astype(F32), axis=0, keepdims=True) for column in (target, arrival)]
    table = jnp.concatenate(rows + [jnp.zeros((6, HD), F32)], axis=0).astype(I32)
    return table, depth


def row_tags(device, holder, hist_ref, pack_ref, hold, block_rows):
    total = holder.shape[1]
    blocks = iota((8, total), 1)
    request = jnp.zeros((8, total), F32)
    for which, start, stop in spans(hist_ref, pack_ref):
        request = jnp.where((blocks >= start) & (blocks < stop), (which + 1).astype(F32), request)
    local = holder - device * hold
    match = local == iota((hold * block_rows, total), 0) // block_rows
    return lax.dot_general(
        request.astype(BF16), match.astype(F32).astype(BF16), (((1,), (1,)), ((), ())), preferred_element_type=F32
    )


def project_kernel(owned, capacity, hist_hbm, pack_hbm, len_hbm, holder_hbm, wave_hbm, new_hbm, rows_hbm, weight_hbm,
                   pairs, table_out, tags, turns,
                   rows_buf, weight_buf, total, fresh, hist_ref, pack_ref, len_ref, holder_ref, wave_ref, new_ref,
                   small_sem, rows_sem, weight_sem):
    hold, block_rows, width = rows_hbm.shape
    small = [
        pltpu.make_async_copy(source, target, small_sem.at[index])
        for index, (source, target) in enumerate((
            (hist_hbm, hist_ref), (pack_hbm, pack_ref), (len_hbm, len_ref), (holder_hbm, holder_ref),
            (wave_hbm, wave_ref), (new_hbm, new_ref),
        ))
    ]
    for copy in small:
        copy.start()
    copies, offset = [], 0
    for part, size in enumerate(split_sizes(width)):
        span = pl.ds(offset, size)
        copies.append((
            offset,
            size,
            pltpu.make_async_copy(weight_hbm.at[span, :], weight_buf.at[span, :], weight_sem.at[part]),
            pltpu.make_async_copy(rows_hbm.at[:, :, span], rows_buf.at[:, :, span], rows_sem.at[part]),
        ))
        offset += size

    def depart(part):
        if part < len(copies):
            for copy in copies[part][2:]:
                copy.start()

    depart(0)
    depart(1)

    def multiply(part, lanes):
        offset, size, _, _ = copies[part]
        left = rows_buf[:, :, offset:offset + size].reshape(hold * block_rows, size)
        product = jnp.dot(left, weight_buf[offset:offset + size, lanes], preferred_element_type=F32)
        return product if part == 0 else total[:, lanes] + product

    def arrive(part):
        for copy in copies[part][2:]:
            copy.wait()
        depart(part + 2)

    everything = slice(0, 2 * HALF)
    for part in range(2):
        arrive(part)
        total[...] = multiply(part, everything)
    for copy in small:
        copy.wait()
    device = lax.axis_index("req")
    holder = holder_ref[...]
    found, depth = places(device, holder, hist_ref, pack_ref, hold, owned, capacity)
    table_out[...] = found
    tags[0:8, :] = row_tags(device, holder, hist_ref, pack_ref, hold, block_rows)
    tags[8:16, :] = row_tags(device ^ 1, holder, hist_ref, pack_ref, hold, block_rows)
    wave = wave_ref[...]
    sign = lane_sign((block_rows, HD))
    angle = (depth * block_rows).astype(F32) * wave
    block_cos, block_sin = jnp.cos(angle)[:, None, :], jnp.sin(angle)[:, None, :]
    angle = iota((block_rows, HD), 0).astype(F32) * wave
    row_cos, row_sin = jnp.cos(angle)[None], jnp.sin(angle)[None]
    cosine = (block_cos * row_cos - block_sin * row_sin).reshape(-1, HD)
    sine = ((block_sin * row_cos + block_cos * row_sin) * sign[None]).reshape(-1, HD)
    tokens = new_ref.shape[0]
    first = device * tokens
    place = iota((block_rows, HD), 0) + (hist_ref[first // NEWT] * block_rows + first % NEWT)
    angle = place.astype(F32) * wave
    new_cos, new_sin = jnp.cos(angle), jnp.sin(angle) * sign
    for group in range(turns.shape[0]):
        request = (first // NEWT) ^ group
        place = iota((8, HD), 0) % tokens + (hist_ref[request] * block_rows + first % NEWT)
        angle = place.astype(F32) * wave
        turns[group, 0] = jnp.cos(angle)
        turns[group, 1] = jnp.sin(angle) * lane_sign((8, HD))
        tags[pl.ds(16 + group, 1), :] = jnp.full((1, tags.shape[1]), len_ref[request].astype(F32))
    fresh[...] = jnp.zeros_like(fresh)
    fresh[0:tokens, :] = new_ref[...].astype(F32)
    for head in range(KVH):
        lanes = slice(head * HD, (head + 1) * HD)
        part = fresh[:, lanes]
        pairs[hold, :, lanes] = (part * new_cos + pltpu.roll(part, HD // 2, 1) * new_sin).astype(BF16)
    pairs[hold, :, HALF:] = fresh[:, HALF:].astype(BF16)
    last = len(copies) - 1
    for part in range(2, last):
        arrive(part)
        total[...] = multiply(part, everything)
    arrive(last)
    for head in range(2 * KVH):
        lanes = slice(head * HD, (head + 1) * HD)
        if head % KVH == 0:
            half = slice(head * HD, (head + KVH) * HD)
            total[:, half] = multiply(last, half)
        part = total[:, lanes]
        if head < KVH:
            part = part * cosine + pltpu.roll(part, HD // 2, 1) * sine
        pairs[0:hold, :, lanes] = part.astype(BF16).reshape(hold, block_rows, HD)


def ship_kernel(groups, table_hbm, pairs, turns, *refs):
    queries, (outgoing, turned, rows, table, table_sem, send_sem) = refs[:groups], refs[groups:]
    table_copy = pltpu.make_async_copy(table_hbm, table, table_sem)
    table_copy.start()
    hold = outgoing.shape[0]
    tokens = queries[0].shape[0]

    def turn(group):
        values = queries[group][...].astype(F32)
        for head in range(KVH * QPK):
            rows[group, pl.ds(head * tokens, tokens), :] = values[:, head * HD:(head + 1) * HD]
        flat = rows[group]
        swapped = pltpu.roll(flat, HD // 2, 1)
        result = flat.reshape(-1, 8, HD) * turns[group, 0][None] + swapped.reshape(-1, 8, HD) * turns[group, 1][None]
        turned[:, group] = result.reshape(KVH, QPK * tokens, HD).astype(BF16)

    for group in range(groups // 2):
        turn(group)
    table_copy.wait()

    def send(slot, carry):
        pltpu.make_async_copy(pairs.at[slot], outgoing.at[table[0, slot]], send_sem).start()
        return carry

    lax.fori_loop(0, hold, send, 0)
    for group in range(groups // 2, groups):
        turn(group)
    pltpu.make_async_copy(pairs.at[pl.ds(0, hold)], outgoing, send_sem).wait()


def encode(level):
    lanes = iota(level.shape, 1)
    high = level.astype(BF16).astype(F32)
    rest = level - high
    middle = rest.astype(BF16).astype(F32)
    low = rest - middle
    packed = jnp.where(lanes < 32, high, jnp.where(lanes < 64, pltpu.roll(middle, 32, 1), pltpu.roll(low, 64, 1)))
    return jnp.where(lanes < 96, packed, 0.0).astype(BF16)


def decode(packed):
    packed = packed.astype(F32)
    return packed + (pltpu.roll(packed, HD - 32, 1) + pltpu.roll(packed, HD - 64, 1))


def folding_order(groups):
    if groups == 1:
        return [0]
    inner = folding_order(groups // 2)
    return [2 * group for group in inner] + [2 * group + 1 for group in inner]


def attend_kernel(groups, tokens, queries, queries_across, pairs, pairs_beside, tags, keep, send):
    hold, block_rows = pairs.shape[0] - 1, pairs.shape[1]
    rows_kept = hold * block_rows
    span = QPK * tokens
    rows = 2 * groups * span
    device = lax.axis_index("req")
    per_request = NEWT // tokens
    request = device // per_request
    row = iota((rows, 1), 0)
    group = (row // span) % groups
    wanted = ((request ^ group) + 1).astype(F32)
    tag_rows = [tags[0:1, :], tags[8:9, :]]
    row_all = iota((rows, 2 * block_rows), 0)
    column = iota((rows, 2 * block_rows), 1)
    across = row_all // (groups * span)
    query_place = ((device ^ (2 * across)) % per_request) * tokens + row_all % tokens
    key_index = column % block_rows
    key_place = ((device ^ (column // block_rows)) % per_request) * tokens + key_index
    fresh_ok = (
        ((row_all // span) % groups == 0) & (key_index < tokens) & (key_place <= query_place)
        & (key_place.astype(F32) < tags[16:17, 0:1])
    )
    limit = jnp.zeros((rows, 1), F32)
    for layer in range(groups):
        limit = jnp.where(group == layer, tags[16 + layer:17 + layer, 0:1], limit)
    side = row // (groups * span)
    live = (((device ^ (2 * side)) % per_request) * tokens + row % tokens).astype(F32) < limit
    lanes = iota((rows, HD), 1)
    levels = jnp.zeros((rows, HD), F32)
    for head in range(KVH):
        key_lanes = slice(head * HD, (head + 1) * HD)
        value_lanes = slice(HALF + head * HD, HALF + (head + 1) * HD)
        query = jnp.concatenate(
            [queries[head].reshape(groups * span, HD), queries_across[head].reshape(groups * span, HD)], axis=0
        )
        scores, values = [], []
        for source, tag in zip((pairs, pairs_beside), tag_rows):
            keys = source[0:hold, :, key_lanes].reshape(rows_kept, HD)
            part = lax.dot_general(query, keys, (((1,), (1,)), ((), ())), preferred_element_type=F32) * SCALE
            scores.append(jnp.where(tag == wanted, part, MASKED))
            values.append(source[0:hold, :, value_lanes].reshape(rows_kept, HD))
        keys = jnp.concatenate([pairs[hold, :, key_lanes], pairs_beside[hold, :, key_lanes]], axis=0)
        part = lax.dot_general(query, keys, (((1,), (1,)), ((), ())), preferred_element_type=F32) * SCALE
        scores.append(jnp.where(fresh_ok, part, MASKED))
        values.append(jnp.concatenate([pairs[hold, :, value_lanes], pairs_beside[hold, :, value_lanes]], axis=0))
        peak = jnp.max(jnp.maximum(scores[0], scores[1]), axis=1, keepdims=True)
        peak = jnp.maximum(peak, jnp.max(scores[2], axis=1, keepdims=True))
        weights = [jnp.exp(part - peak) for part in scores]
        denominator = lane_total(weights[0] + weights[1]) + lane_total(weights[2])
        sums = None
        for weight, value in zip(weights, values):
            part = jnp.dot(weight.astype(BF16), value, preferred_element_type=F32)
            sums = part if sums is None else sums + part
        sums = jnp.where(live, sums / denominator, 0.0).astype(BF16).reshape(2, groups, span, HD)
        for place, group in enumerate(folding_order(groups)):
            keep[place, head] = sums[0, group]
            send[place, head] = sums[1, group]
        levels = jnp.where(lanes == head, peak + jnp.log(denominator), levels)
    packed = encode(levels).reshape(2, groups, span, HD)
    for place, group in enumerate(folding_order(groups)):
        keep[place, KVH] = packed[0, group]
        send[place, KVH] = packed[1, group]


def merge(parts):
    levels = [decode(part[KVH]) for part in parts]
    top = functools.reduce(jnp.maximum, levels)
    scales = [jnp.exp(level - top) for level in levels]
    whole = functools.reduce(jnp.add, scales)
    scales = [scale / whole for scale in scales]
    heads = []
    for head in range(KVH):
        pieces = [part[head].astype(F32) * scale[:, head:head + 1] for part, scale in zip(parts, scales)]
        heads.append(functools.reduce(jnp.add, pieces))
    return heads, top + jnp.log(whole)


def fold_kernel(kept, received, keep, send):
    count = kept.shape[0]
    for group in range(count):
        heads, level = merge([kept[group], received[group]])
        out, index = (keep, group) if group < count // 2 else (send, group - count // 2)
        for head in range(KVH):
            out[index, head] = heads[head].astype(BF16)
        out[index, KVH] = encode(level)


def finish_kernel(tokens, *refs):
    parts, out = refs[:-1], refs[-1]
    heads, _ = merge([part[0] for part in parts])
    for head in range(KVH):
        for inner in range(QPK):
            start = (head * QPK + inner) * HD
            out[:, start:start + HD] = heads[head][inner * tokens:(inner + 1) * tokens, :].astype(BF16)


def settle_kernel(table, incoming, out, sem):
    def place(block, carry):
        pltpu.make_async_copy(incoming.at[table[1, block]], out.at[block], sem).start()
        return carry

    lax.fori_loop(0, out.shape[0], place, 0)
    pltpu.make_async_copy(incoming.at[pl.ds(0, out.shape[0])], out, sem).wait()


def on_device(
    saved_hidden, kv_weight, queries, new_kv, hist_blocks, new_len, pack_order, holder_slot
):
    count = lax.axis_size("req")
    hold, block_rows, width = saved_hidden.shape
    pair_width = kv_weight.shape[1]
    owned = holder_slot.shape[0] // count
    capacity = hold // count
    tokens, query_width = queries.shape
    groups = count // LAYER
    span = QPK * tokens
    wave = jnp.asarray(frequencies())

    def swap(value, flip):
        return lax.ppermute(value, "req", [(i, i ^ flip) for i in range(count)])

    layers = [queries] + [swap(queries, LAYER * group) for group in range(1, groups)]
    chunks = len(split_sizes(width))
    pairs, table, tags, turns = call(
        functools.partial(project_kernel, owned, capacity),
        "project",
        tuple(
            pltpu.with_memory_space_constraint(value, HBM)
            for value in (
                hist_blocks, pack_order, new_len, holder_slot.reshape(1, -1), wave, new_kv, saved_hidden, kv_weight
            )
        ),
        (HBM,) * 8,
        (
            ((hold + 1, block_rows, pair_width), BF16),
            ((8, HD), I32),
            ((16 + groups, hold * block_rows), F32),
            ((groups, 2, 8, HD), F32),
        ),
        (VM,) * 4,
        (
            VM((hold, block_rows, width), BF16),
            VM((width, pair_width), BF16),
            VM((hold * block_rows, pair_width), F32),
            VM((block_rows, pair_width), F32),
            SM(hist_blocks.shape, I32),
            SM(pack_order.shape, I32),
            SM(new_len.shape, I32),
            VM((1, holder_slot.shape[0]), I32),
            VM(wave.shape, F32),
            VM(new_kv.shape, BF16),
            pltpu.SemaphoreType.DMA((6,)),
            pltpu.SemaphoreType.DMA((chunks,)),
            pltpu.SemaphoreType.DMA((chunks,)),
        ),
        34,
    )
    outgoing, turned = call(
        functools.partial(ship_kernel, groups),
        "ship",
        (table, pairs, turns, *layers),
        (ANY,) + (VM,) * (groups + 2),
        (
            ((hold, block_rows, pair_width), BF16),
            ((KVH, groups, span, HD), BF16),
        ),
        (ANY, VM),
        (
            VM((groups, KVH * span, HD), F32),
            SM((8, HD), I32),
            pltpu.SemaphoreType.DMA(()),
            pltpu.SemaphoreType.DMA(()),
        ),
    )
    outgoing, pairs, turned = lax.optimization_barrier((outgoing, pairs, turned))
    pairs_beside = swap(pairs, 1)
    turned_across = swap(turned, 2)
    incoming = lax.all_to_all(outgoing, "req", split_axis=0, concat_axis=0, tiled=True)
    share = ((groups, KVH + 1, span, HD), BF16)
    keep, send = call(
        functools.partial(attend_kernel, groups, tokens),
        "attend",
        (turned, turned_across, pairs, pairs_beside, tags),
        (VM,) * 5,
        (share, share),
        (VM, VM),
        mib=24,
        work=ATTEND_WORK,
    )
    step, left = 2, groups
    while left > 1:
        left //= 2
        share = ((left, KVH + 1, span, HD), BF16)
        keep, send = call(fold_kernel, "fold", (keep, swap(send, step)), (VM, VM), (share, share), (VM, VM))
        step *= 2
    parts = [keep, swap(send, step)]
    (restored,) = call(
        settle_kernel,
        "settle",
        (table, incoming),
        (SM, ANY),
        (((owned, block_rows, pair_width), BF16),),
        (ANY,),
        (pltpu.SemaphoreType.DMA(()),),
    )
    parts, restored = lax.optimization_barrier((parts, restored))
    (attention,) = call(
        functools.partial(finish_kernel, tokens),
        "finish",
        tuple(parts),
        (VM, VM),
        (((tokens, query_width), BF16),),
        (VM,),
    )
    return restored, attention


def solution(mesh):
    return jax.shard_map(
        on_device,
        mesh=mesh,
        in_specs=(
            P(("groups", "req"), None, None),
            P(),
            P(("groups", "req"), None),
            P(("groups", "req"), None),
            P("groups"),
            P("groups"),
            P("groups"),
            P("groups"),
        ),
        out_specs=(P(("groups", "req"), None, None), P(("groups", "req"), None)),
        check_vma=False,
    )
```

time: 261 us -> 56.1 us (0.21)
  blocking collectives: 159 us -> 0 us
  Pallas kernels: 0 us -> 19.5 us
  between operations: 19.4 us -> 0.74 us
  local copies, waits for them, and re-layouts: 18 us -> 0.01 us
  matrix products: 15.1 us -> 0 us
  other arithmetic: 13.1 us -> 0 us
  starting transfers between devices: 7.42 us -> 18.7 us
  loops' own time: 9.65 us -> 0 us
  waiting for transfers between devices: 21.3 us -> 16.9 us
    pmax x1 -> x0, blocking collectives: 74.7 us -> none  [on_device(): global_peak = lax.pmax(peaks, 'req')]
    all_gather x2 -> x0, blocking collectives: 53.8 us -> none  [the longest x1 31.9 us: on_device(): lax.all_gather(queries, 'req', axis=0, tiled=True)]
    unnamed x1 -> x0, blocking collectives: 30.1 us -> none
    reduce_scatter x1 -> x0, waiting for transfers between devices: 21.3 us -> none  [on_device(): lax.psum_scatter((numerators * factor[..., None]).astype(jnp.bfloat16), '...]
    pallas_call x0 -> x7, Pallas kernels: none -> 19.5 us  [call(): pl.pallas_call(kernel, out_shape=tuple((jax.ShapeDtypeStruct(shape, kind)...]
    ppermute x0 -> x8, waiting for transfers between devices: none -> 16.9 us  [swap(): return lax.ppermute(value, 'req', [(i, i ^ flip) for i in range(count)])]
    dot_general x3 -> x0, matrix products: 15.1 us -> none  [the longest x1 14.4 us: on_device(): jnp.einsum('ibd,dc->ibc', outgoing, kv_weight, preferred_element_type=jnp...]
    ppermute x0 -> x8, starting transfers between devices: none -> 13.8 us  [swap(): return lax.ppermute(value, 'req', [(i, i ^ flip) for i in range(count)])]
  transfers between devices with their start and end apart: 2 -> 9, of which waited for: 1 -> 3; matrix products, arithmetic and copies ran while one was open for 1% -> 0% of each run, Pallas kernels for 0% -> 31%
where the time goes in v1:
time: 56.1 us; the launch traced here: 55.9 us
  Pallas kernels  19.5 us (35%)
  starting transfers between devices  18.7 us (33%)
  waiting for transfers between devices  16.9 us (30%)
  between operations  0.74 us (1%)
    pallas_call x7, Pallas kernels, call(): pl.pallas_call(kernel, out_shape=tuple((jax.ShapeDtypeStruct(shape, kind)...  19.5 us
    ppermute x8, waiting for transfers between devices, swap(): return lax.ppermute(value, 'req', [(i, i ^ flip) for i in range(count)])  16.9 us
    ppermute x8, starting transfers between devices, swap(): return lax.ppermute(value, 'req', [(i, i ^ flip) for i in range(count)])  13.8 us
    all_to_all x1, starting transfers between devices, on_device(): lax.all_to_all(outgoing, 'req', split_axis=0, concat_axis=0, tiled=True)  4.98 us
  transfers between devices with their start and end apart: 9, of which 3 were waited for; matrix products, arithmetic and copies ran while one was open for 0% of the time, Pallas kernels for 31%

profile of v1, /device:TPU:0, one launch (start us, length us, event | category | flops | bytes accessed | tf_op | source)
XLA Modules:
  0.0 55.9 jit_solution(3299530972411166525)
XLA Ops:
  0.6 4.1 %collective-permute-start.1 = (bf16[4,4096]{1,0:T(4,128)(2,1)}, bf16[4,4096]{1,0:T(4,128)(2,1)S(1)}, u32[]{:S(2)}, u32[]{:S(2)}) collective-permute-start(bf16[4,4096]{1,0:T(4,128)(2,1)} %refs_0_.1), channel_id=1, source_target_pairs={{0,8},{1,9},{2,10},{3,11},{4,12},{5,13},{6,14},{7,15},{8,0},{9,1},... | collective-permute-start | bytes 98312 | tf_op jit(solution)/shard_map/ppermute | solution.py:389
  4.7 1.6 %collective-permute-start = (bf16[4,4096]{1,0:T(4,128)(2,1)}, bf16[4,4096]{1,0:T(4,128)(2,1)S(1)}, u32[]{:S(2)}, u32[]{:S(2)}) collective-permute-start(bf16[4,4096]{1,0:T(4,128)(2,1)} %refs_0_.1), channel_id=1, source_target_pairs={{0,4},{1,5},{2,6},{3,7},{4,0},{5,1},{6,2},{7,3},{8,12},{9,13},{10,... | collective-permute-start | bytes 98312 | tf_op jit(solution)/shard_map/ppermute | solution.py:389
  6.3 0.0 collective-permute-start.2
  6.3 0.0 copy-start
  6.3 11.9 %project.1 = (bf16[65,8,1024]{2,1,0:T(8,128)(2,1)S(1)}, s32[8,128]{1,0:T(8,128)S(1)}, f32[20,512]{1,0:T(8,128)S(1)}, f32[4,2,8,128]{3,2,1,0:T(8,128)S(1)}) custom-call(s32[4]{0:T(128)} %hist_hbm.1, s32[4]{0:T(128)} %pack_hbm.1, s32[4]{0:T(128)} %len_hbm.1, s32[1,512]{1,0:T(1,128)} %bitcast.1, f32[1,128]{1,0:T(1,128)} %constant.2.clone.wave_hbm, ...), custom_call_target="tpu_custom_call" | custom-call | tf_op jit(solution)/shard_map/project/pallas_call | solution.py:45
  18.2 0.0 collective-permute-done.1.refs_2_
  18.2 0.0 collective-permute-done.refs_1_
  18.2 0.0 collective-permute-done.2.refs_3_
  18.2 0.0 copy-done
  18.2 1.6 %ship.1 = (bf16[64,8,1024]{2,1,0:T(8,128)(2,1)}, bf16[4,4,32,128]{3,2,1,0:T(8,128)(2,1)S(1)}) custom-call(s32[8,128]{1,0:T(8,128)S(1)} %get-tuple-element.20.table_hbm.table, bf16[65,8,1024]{2,1,0:T(8,128)(2,1)S(1)} %get-tuple-element.26.pairs, f32[4,2,8,128]{3,2,1,0:T(8,128)S(1)} %get-tuple-element.22.turns, bf16[4,4096]{1,0:T(4,128)(2,1)S(1)} %copy-done, ...), custom_call_target="tpu_custom_call" | custom-call | tf_op jit(solution)/shard_map/ship/pallas_call | solution.py:45
  19.8 0.1 collective-permute-start.4
  19.9 1.8 %collective-permute-start.3 = (bf16[4,4,32,128]{3,2,1,0:T(8,128)(2,1)S(1)}, bf16[4,4,32,128]{3,2,1,0:T(8,128)(2,1)S(1)}, u32[]{:S(2)}, u32[]{:S(2)}) collective-permute-start(bf16[4,4,32,128]{3,2,1,0:T(8,128)(2,1)S(1)} %get-tuple-element.25.queries), channel_id=1, source_target_pairs={{0,2},{1,3},{2,0},{3,1},{4,6},{5,7},{6,4},{7,5},{8,10},{9,11},{10,... | collective-permute-start | bytes 393224 | tf_op jit(solution)/shard_map/ppermute | solution.py:389
  21.7 5.0 %all-to-all-start = ((bf16[64,8,1024]{2,1,0:T(8,128)(2,1)}), bf16[64,8,1024]{2,1,0:T(8,128)(2,1)S(1)}, u32[]{:S(2)}, u32[]{:S(2)}) async-start(bf16[64,8,1024]{2,1,0:T(8,128)(2,1)} %get-tuple-element.34), calls=%async_computation | async-start | bytes 2097152 | tf_op jit(solution)/shard_map/all_to_all | solution.py:447
  26.7 0.0 collective-permute-done.3.queries_across
  26.7 0.0 collective-permute-done.4.pairs_beside
  26.8 2.9 %attend.1 = (bf16[4,5,32,128]{3,2,1,0:T(8,128)(2,1)S(1)}, bf16[4,5,32,128]{3,2,1,0:T(8,128)(2,1)S(1)}) custom-call(bf16[4,4,32,128]{3,2,1,0:T(8,128)(2,1)S(1)} %get-tuple-element.25.queries, bf16[4,4,32,128]{3,2,1,0:T(8,128)(2,1)S(1)} %collective-permute-done.3.queries_across, bf16[65,8,1024]{2,1,0:T(8,128)(2,1)S(1)} %get-tuple-element.26.pairs, ...), custom_call_target="tpu_custom_call" | custom-call | flops 60000002048 | tf_op jit(solution)/shard_map/attend/pallas_call | solution.py:45
  29.7 2.0 %collective-permute-start.5 = (bf16[4,5,32,128]{3,2,1,0:T(8,128)(2,1)S(1)}, bf16[4,5,32,128]{3,2,1,0:T(8,128)(2,1)S(1)}, u32[]{:S(2)}, u32[]{:S(2)}) collective-permute-start(bf16[4,5,32,128]{3,2,1,0:T(8,128)(2,1)S(1)} %get-tuple-element.29), channel_id=1, source_target_pairs={{0,2},{1,3},{2,0},{3,1},{4,6},{5,7},{6,4},{7,5},{8,10},{9,11},{10,... | collective-permute-start | bytes 491528 | tf_op jit(solution)/shard_map/ppermute | solution.py:389
  31.7 10.1 %collective-permute-done.5.received = bf16[4,5,32,128]{3,2,1,0:T(8,128)(2,1)S(1)} collective-permute-done((bf16[4,5,32,128]{3,2,1,0:T(8,128)(2,1)S(1)}, bf16[4,5,32,128]{3,2,1,0:T(8,128)(2,1)S(1)}, u32[]{:S(2)}, u32[]{:S(2)}) %collective-permute-start.5) | collective-permute-done | bytes 163872 | tf_op jit(solution)/shard_map/ppermute | solution.py:389
  41.8 0.6 %fold.2 = (bf16[2,5,32,128]{3,2,1,0:T(8,128)(2,1)S(1)}, bf16[2,5,32,128]{3,2,1,0:T(8,128)(2,1)S(1)}) custom-call(bf16[4,5,32,128]{3,2,1,0:T(8,128)(2,1)S(1)} %get-tuple-element.28.kept, bf16[4,5,32,128]{3,2,1,0:T(8,128)(2,1)S(1)} %collective-permute-done.5.received), custom_call_target="tpu_custom_call" | custom-call | tf_op jit(solution)/shard_map/fold/pallas_call | solution.py:45
  42.4 0.1 collective-permute-start.6
  42.5 4.4 %collective-permute-done.6.received = bf16[2,5,32,128]{3,2,1,0:T(8,128)(2,1)S(1)} collective-permute-done((bf16[2,5,32,128]{3,2,1,0:T(8,128)(2,1)S(1)}, bf16[2,5,32,128]{3,2,1,0:T(8,128)(2,1)S(1)}, u32[]{:S(2)}, u32[]{:S(2)}) %collective-permute-start.6) | collective-permute-done | bytes 81952 | tf_op jit(solution)/shard_map/ppermute | solution.py:389
  46.9 0.3 fold.3
  47.2 4.1 %collective-permute-start.7 = (bf16[1,5,32,128]{3,2,1,0:T(8,128)(2,1)S(1)}, bf16[1,5,32,128]{3,2,1,0:T(8,128)(2,1)S(1)}, u32[]{:S(2)}, u32[]{:S(2)}) collective-permute-start(bf16[1,5,32,128]{3,2,1,0:T(8,128)(2,1)S(1)} %get-tuple-element.33), channel_id=1, source_target_pairs={{0,8},{1,9},{2,10},{3,11},{4,12},{5,13},{6,14},{7,15},{8,0},{9,1},... | collective-permute-start | bytes 122888 | tf_op jit(solution)/shard_map/ppermute | solution.py:389
  51.3 0.0 all-to-all-done.incoming
  51.3 1.4 %settle.1 = bf16[32,8,1024]{2,1,0:T(8,128)(2,1)} custom-call(s32[8,128]{1,0:T(8,128)S(1)} %get-tuple-element.20.table_hbm.table, bf16[64,8,1024]{2,1,0:T(8,128)(2,1)S(1)} %all-to-all-done.incoming), custom_call_target="tpu_custom_call" | custom-call | tf_op jit(solution)/shard_map/settle/pallas_call | solution.py:45
  52.8 2.3 %collective-permute-done.7.refs_1_ = bf16[1,5,32,128]{3,2,1,0:T(8,128)(2,1)S(1)} collective-permute-done((bf16[1,5,32,128]{3,2,1,0:T(8,128)(2,1)S(1)}, bf16[1,5,32,128]{3,2,1,0:T(8,128)(2,1)S(1)}, u32[]{:S(2)}, u32[]{:S(2)}) %collective-permute-start.7) | collective-permute-done | bytes 40992 | tf_op jit(solution)/shard_map/ppermute | solution.py:389
  55.0 0.8 %finish.1 = bf16[4,4096]{1,0:T(4,128)(2,1)} custom-call(bf16[1,5,32,128]{3,2,1,0:T(8,128)(2,1)S(1)} %get-tuple-element.36.refs_0_, bf16[1,5,32,128]{3,2,1,0:T(8,128)(2,1)S(1)} %collective-permute-done.7.refs_1_), custom_call_target="tpu_custom_call" | custom-call | tf_op jit(solution)/shard_map/finish/pallas_call | solution.py:45
Async XLA Ops:
  0.6 17.6 %collective-permute-start.1 = (bf16[4,4096]{1,0:T(4,128)(2,1)}, bf16[4,4096]{1,0:T(4,128)(2,1)S(1)}, u32[]{:S(2)}, u32[]{:S(2)}) collective-permute-start(bf16[4,4096]{1,0:T(4,128)(2,1)} %refs_0_.1), channel_id=1, source_target_pairs={{0,8},{1,9},{2,10},{3,11},{4,12},{5,13},{6,14},{7,15},{8,0},{9,1},... | collective-permute-start | bytes 98312 | tf_op jit(solution)/shard_map/ppermute | solution.py:389
  4.7 13.5 %collective-permute-start = (bf16[4,4096]{1,0:T(4,128)(2,1)}, bf16[4,4096]{1,0:T(4,128)(2,1)S(1)}, u32[]{:S(2)}, u32[]{:S(2)}) collective-permute-start(bf16[4,4096]{1,0:T(4,128)(2,1)} %refs_0_.1), channel_id=1, source_target_pairs={{0,4},{1,5},{2,6},{3,7},{4,0},{5,1},{6,2},{7,3},{8,12},{9,13},{10,... | collective-permute-start | bytes 98312 | tf_op jit(solution)/shard_map/ppermute | solution.py:389
  6.3 11.9 %collective-permute-start.2 = (bf16[4,4096]{1,0:T(4,128)(2,1)}, bf16[4,4096]{1,0:T(4,128)(2,1)S(1)}, u32[]{:S(2)}, u32[]{:S(2)}) collective-permute-start(bf16[4,4096]{1,0:T(4,128)(2,1)} %refs_0_.1), channel_id=1, source_target_pairs={{0,12},{1,13},{2,14},{3,15},{4,8},{5,9},{6,10},{7,11},{8,4},{9,5},... | collective-permute-start | bytes 98312 | tf_op jit(solution)/shard_map/ppermute | solution.py:389
  6.3 11.9 %copy-start = (bf16[4,4096]{1,0:T(4,128)(2,1)S(1)}, bf16[4,4096]{1,0:T(4,128)(2,1)}, u32[]{:S(2)}) copy-start(bf16[4,4096]{1,0:T(4,128)(2,1)} %refs_0_.1) | copy-start | bytes 98308
  19.8 6.9 %collective-permute-start.4 = (bf16[65,8,1024]{2,1,0:T(8,128)(2,1)S(1)}, bf16[65,8,1024]{2,1,0:T(8,128)(2,1)S(1)}, u32[]{:S(2)}, u32[]{:S(2)}) collective-permute-start(bf16[65,8,1024]{2,1,0:T(8,128)(2,1)S(1)} %get-tuple-element.26.pairs), channel_id=1, source_target_pairs={{0,1},{1,0},{2,3},{3,2},{4,5},{5,4},{6,7},{7,6},{8,9},{9,8},{10,11... | collective-permute-start | bytes 3194888 | tf_op jit(solution)/shard_map/ppermute | solution.py:389
  19.9 6.8 %collective-permute-start.3 = (bf16[4,4,32,128]{3,2,1,0:T(8,128)(2,1)S(1)}, bf16[4,4,32,128]{3,2,1,0:T(8,128)(2,1)S(1)}, u32[]{:S(2)}, u32[]{:S(2)}) collective-permute-start(bf16[4,4,32,128]{3,2,1,0:T(8,128)(2,1)S(1)} %get-tuple-element.25.queries), channel_id=1, source_target_pairs={{0,2},{1,3},{2,0},{3,1},{4,6},{5,7},{6,4},{7,5},{8,10},{9,11},{10,... | collective-permute-start | bytes 393224 | tf_op jit(solution)/shard_map/ppermute | solution.py:389
  21.7 29.6 %all-to-all-start = ((bf16[64,8,1024]{2,1,0:T(8,128)(2,1)}), bf16[64,8,1024]{2,1,0:T(8,128)(2,1)S(1)}, u32[]{:S(2)}, u32[]{:S(2)}) async-start(bf16[64,8,1024]{2,1,0:T(8,128)(2,1)} %get-tuple-element.34), calls=%async_computation | async-start | bytes 2097152 | tf_op jit(solution)/shard_map/all_to_all | solution.py:447
  29.7 12.1 %collective-permute-start.5 = (bf16[4,5,32,128]{3,2,1,0:T(8,128)(2,1)S(1)}, bf16[4,5,32,128]{3,2,1,0:T(8,128)(2,1)S(1)}, u32[]{:S(2)}, u32[]{:S(2)}) collective-permute-start(bf16[4,5,32,128]{3,2,1,0:T(8,128)(2,1)S(1)} %get-tuple-element.29), channel_id=1, source_target_pairs={{0,2},{1,3},{2,0},{3,1},{4,6},{5,7},{6,4},{7,5},{8,10},{9,11},{10,... | collective-permute-start | bytes 491528 | tf_op jit(solution)/shard_map/ppermute | solution.py:389
  42.4 4.5 %collective-permute-start.6 = (bf16[2,5,32,128]{3,2,1,0:T(8,128)(2,1)S(1)}, bf16[2,5,32,128]{3,2,1,0:T(8,128)(2,1)S(1)}, u32[]{:S(2)}, u32[]{:S(2)}) collective-permute-start(bf16[2,5,32,128]{3,2,1,0:T(8,128)(2,1)S(1)} %get-tuple-element.31), channel_id=1, source_target_pairs={{0,4},{1,5},{2,6},{3,7},{4,0},{5,1},{6,2},{7,3},{8,12},{9,13},{10,... | collective-permute-start | bytes 245768 | tf_op jit(solution)/shard_map/ppermute | solution.py:389
  47.2 7.9 %collective-permute-start.7 = (bf16[1,5,32,128]{3,2,1,0:T(8,128)(2,1)S(1)}, bf16[1,5,32,128]{3,2,1,0:T(8,128)(2,1)S(1)}, u32[]{:S(2)}, u32[]{:S(2)}) collective-permute-start(bf16[1,5,32,128]{3,2,1,0:T(8,128)(2,1)S(1)} %get-tuple-element.33), channel_id=1, source_target_pairs={{0,8},{1,9},{2,10},{3,11},{4,12},{5,13},{6,14},{7,15},{8,0},{9,1},... | collective-permute-start | bytes 122888 | tf_op jit(solution)/shard_map/ppermute | solution.py:389

commit v2 on v1

--- a/solution.py
+++ b/solution.py
@@ -84,7 +84,7 @@
     block = lane_total(jnp.where(here, blocks, 0).astype(F32)).astype(I32)
     owner = block // owned
     rank = lane_total(jnp.where(held & (blocks < block) & (blocks >= owner * owned), 1.0, 0.0)).astype(I32)
-    target = jnp.minimum(owner * capacity + jnp.minimum(rank, capacity - 1), hold - 1)
+    target = jnp.clip(hold - (owner + 1) * capacity + jnp.minimum(rank, capacity - 1), 0, hold - 1)
     target = jnp.where(lane_total(jnp.where(here, 1.0, 0.0)) > 0, target, iota((hold, 1), 0))
     depth = jnp.zeros((hold, 1), I32)
     for _, start, stop in spans(hist_ref, pack_ref):
@@ -95,7 +95,7 @@
     keeper = holder // hold
     kept = lane_total(jnp.where(blocks == rows, keeper, 0).astype(F32)).astype(I32)
     order = lane_total(jnp.where((keeper == kept) & (blocks >= mine) & (blocks < rows), 1.0, 0.0)).astype(I32)
-    arrival = kept * capacity + jnp.minimum(order, capacity - 1)
+    arrival = hold - (kept + 1) * capacity + jnp.minimum(order, capacity - 1)
     arrival = jnp.concatenate([arrival, jnp.zeros((hold - owned, 1), I32)], axis=0)
     diagonal = iota((hold, HD), 0) == iota((hold, HD), 1)
     rows = [jnp.sum(jnp.where(diagonal, column, 0).astype(F32), axis=0, keepdims=True) for column in (target, arrival)]
@@ -444,7 +444,10 @@
     outgoing, pairs, turned = lax.optimization_barrier((outgoing, pairs, turned))
     pairs_beside = swap(pairs, 1)
     turned_across = swap(turned, 2)
-    incoming = lax.all_to_all(outgoing, "req", split_axis=0, concat_axis=0, tiled=True)
+    backwards = [list(range(count))[::-1]]
+    incoming = lax.all_to_all(
+        outgoing, "req", split_axis=0, concat_axis=0, axis_index_groups=backwards, tiled=True
+    )
     share = ((groups, KVH + 1, span, HD), BF16)
     keep, send = call(
         functools.partial(attend_kernel, groups, tokens),

time: 56.1 us -> 55.1 us (0.982)
  starting transfers between devices: 18.7 us -> 16.7 us
  waiting for transfers between devices: 16.9 us -> 18 us
    ppermute x8, starting transfers between devices: 13.8 us -> 9.76 us  [swap(): return lax.ppermute(value, 'req', [(i, i ^ flip) for i in range(count)])]
    all_to_all x1, waiting for transfers between devices: 0.01 us -> 2.38 us  [on_device(): lax.all_to_all(outgoing, 'req', split_axis=0, concat_axis=0, axis_index_g...]
    all_to_all x1, starting transfers between devices: 4.98 us -> 6.89 us  [on_device(): lax.all_to_all(outgoing, 'req', split_axis=0, concat_axis=0, axis_index_g...]
    ppermute x8, waiting for transfers between devices: 16.9 us -> 15.7 us  [swap(): return lax.ppermute(value, 'req', [(i, i ^ flip) for i in range(count)])]
  transfers between devices with their start and end apart: 9 -> 9, of which waited for: 3 -> 4; matrix products, arithmetic and copies ran while one was open for 0% -> 0% of each run, Pallas kernels for 31% -> 31%
where the time goes in v2:
time: 55.1 us; the launch traced here: 54.9 us
  Pallas kernels  19.5 us (35%)
  waiting for transfers between devices  18 us (33%)
  starting transfers between devices  16.7 us (30%)
  between operations  0.73 us (1%)
    pallas_call x7, Pallas kernels, call(): pl.pallas_call(kernel, out_shape=tuple((jax.ShapeDtypeStruct(shape, kind)...  19.5 us
    ppermute x8, waiting for transfers between devices, swap(): return lax.ppermute(value, 'req', [(i, i ^ flip) for i in range(count)])  15.7 us
    ppermute x8, starting transfers between devices, swap(): return lax.ppermute(value, 'req', [(i, i ^ flip) for i in range(count)])  9.76 us
    all_to_all x1, starting transfers between devices, on_device(): lax.all_to_all(outgoing, 'req', split_axis=0, concat_axis=0, axis_index_g...  6.89 us
    all_to_all x1, waiting for transfers between devices, on_device(): lax.all_to_all(outgoing, 'req', split_axis=0, concat_axis=0, axis_index_g...  2.38 us
  transfers between devices with their start and end apart: 9, of which 4 were waited for; matrix products, arithmetic and copies ran while one was open for 0% of the time, Pallas kernels for 31%

profile of v2, /device:TPU:0, one launch (start us, length us, event | category | flops | bytes accessed | tf_op | source)
XLA Modules:
  0.0 54.9 jit_solution(617444733998359629)
XLA Ops:
  0.6 4.1 %collective-permute-start.1 = (bf16[4,4096]{1,0:T(4,128)(2,1)}, bf16[4,4096]{1,0:T(4,128)(2,1)S(1)}, u32[]{:S(2)}, u32[]{:S(2)}) collective-permute-start(bf16[4,4096]{1,0:T(4,128)(2,1)} %refs_0_.1), channel_id=1, source_target_pairs={{0,8},{1,9},{2,10},{3,11},{4,12},{5,13},{6,14},{7,15},{8,0},{9,1},... | collective-permute-start | bytes 98312 | tf_op jit(solution)/shard_map/ppermute | solution.py:389
  4.7 1.6 %collective-permute-start = (bf16[4,4096]{1,0:T(4,128)(2,1)}, bf16[4,4096]{1,0:T(4,128)(2,1)S(1)}, u32[]{:S(2)}, u32[]{:S(2)}) collective-permute-start(bf16[4,4096]{1,0:T(4,128)(2,1)} %refs_0_.1), channel_id=1, source_target_pairs={{0,4},{1,5},{2,6},{3,7},{4,0},{5,1},{6,2},{7,3},{8,12},{9,13},{10,... | collective-permute-start | bytes 98312 | tf_op jit(solution)/shard_map/ppermute | solution.py:389
  6.3 0.0 collective-permute-start.2
  6.3 0.0 copy-start
  6.3 11.9 %project.1 = (bf16[65,8,1024]{2,1,0:T(8,128)(2,1)S(1)}, s32[8,128]{1,0:T(8,128)S(1)}, f32[20,512]{1,0:T(8,128)S(1)}, f32[4,2,8,128]{3,2,1,0:T(8,128)S(1)}) custom-call(s32[4]{0:T(128)} %hist_hbm.1, s32[4]{0:T(128)} %pack_hbm.1, s32[4]{0:T(128)} %len_hbm.1, s32[1,512]{1,0:T(1,128)} %bitcast.1, f32[1,128]{1,0:T(1,128)} %constant.2.clone.wave_hbm, ...), custom_call_target="tpu_custom_call" | custom-call | tf_op jit(solution)/shard_map/project/pallas_call | solution.py:45
  18.2 0.0 collective-permute-done.1.refs_2_
  18.2 0.0 collective-permute-done.refs_1_
  18.2 0.0 collective-permute-done.2.refs_3_
  18.2 0.0 copy-done
  18.2 1.6 %ship.1 = (bf16[64,8,1024]{2,1,0:T(8,128)(2,1)}, bf16[4,4,32,128]{3,2,1,0:T(8,128)(2,1)S(1)}) custom-call(s32[8,128]{1,0:T(8,128)S(1)} %get-tuple-element.20.table_hbm.table, bf16[65,8,1024]{2,1,0:T(8,128)(2,1)S(1)} %get-tuple-element.26.pairs, f32[4,2,8,128]{3,2,1,0:T(8,128)S(1)} %get-tuple-element.22.turns, bf16[4,4096]{1,0:T(4,128)(2,1)S(1)} %copy-done, ...), custom_call_target="tpu_custom_call" | custom-call | tf_op jit(solution)/shard_map/ship/pallas_call | solution.py:45
  19.9 0.1 collective-permute-start.4
  20.0 1.8 %collective-permute-start.3 = (bf16[4,4,32,128]{3,2,1,0:T(8,128)(2,1)S(1)}, bf16[4,4,32,128]{3,2,1,0:T(8,128)(2,1)S(1)}, u32[]{:S(2)}, u32[]{:S(2)}) collective-permute-start(bf16[4,4,32,128]{3,2,1,0:T(8,128)(2,1)S(1)} %get-tuple-element.25.queries), channel_id=1, source_target_pairs={{0,2},{1,3},{2,0},{3,1},{4,6},{5,7},{6,4},{7,5},{8,10},{9,11},{10,... | collective-permute-start | bytes 393224 | tf_op jit(solution)/shard_map/ppermute | solution.py:389
  21.8 6.9 %all-to-all-start = ((bf16[64,8,1024]{2,1,0:T(8,128)(2,1)}), bf16[64,8,1024]{2,1,0:T(8,128)(2,1)S(1)}, u32[]{:S(2)}, u32[]{:S(2)}) async-start(bf16[64,8,1024]{2,1,0:T(8,128)(2,1)} %get-tuple-element.34), calls=%async_computation | async-start | bytes 2097152 | tf_op jit(solution)/shard_map/all_to_all | solution.py:448
  28.6 0.0 collective-permute-done.3.queries_across
  28.7 0.0 collective-permute-done.4.pairs_beside
  28.7 2.9 %attend.1 = (bf16[4,5,32,128]{3,2,1,0:T(8,128)(2,1)S(1)}, bf16[4,5,32,128]{3,2,1,0:T(8,128)(2,1)S(1)}) custom-call(bf16[4,4,32,128]{3,2,1,0:T(8,128)(2,1)S(1)} %get-tuple-element.25.queries, bf16[4,4,32,128]{3,2,1,0:T(8,128)(2,1)S(1)} %collective-permute-done.3.queries_across, bf16[65,8,1024]{2,1,0:T(8,128)(2,1)S(1)} %get-tuple-element.26.pairs, ...), custom_call_target="tpu_custom_call" | custom-call | flops 60000002048 | tf_op jit(solution)/shard_map/attend/pallas_call | solution.py:45
  31.6 0.6 %collective-permute-start.5 = (bf16[4,5,32,128]{3,2,1,0:T(8,128)(2,1)S(1)}, bf16[4,5,32,128]{3,2,1,0:T(8,128)(2,1)S(1)}, u32[]{:S(2)}, u32[]{:S(2)}) collective-permute-start(bf16[4,5,32,128]{3,2,1,0:T(8,128)(2,1)S(1)} %get-tuple-element.29), channel_id=1, source_target_pairs={{0,2},{1,3},{2,0},{3,1},{4,6},{5,7},{6,4},{7,5},{8,10},{9,11},{10,... | collective-permute-start | bytes 491528 | tf_op jit(solution)/shard_map/ppermute | solution.py:389
  32.2 9.7 %collective-permute-done.5.received = bf16[4,5,32,128]{3,2,1,0:T(8,128)(2,1)S(1)} collective-permute-done((bf16[4,5,32,128]{3,2,1,0:T(8,128)(2,1)S(1)}, bf16[4,5,32,128]{3,2,1,0:T(8,128)(2,1)S(1)}, u32[]{:S(2)}, u32[]{:S(2)}) %collective-permute-start.5) | collective-permute-done | bytes 163872 | tf_op jit(solution)/shard_map/ppermute | solution.py:389
  41.9 0.6 %fold.2 = (bf16[2,5,32,128]{3,2,1,0:T(8,128)(2,1)S(1)}, bf16[2,5,32,128]{3,2,1,0:T(8,128)(2,1)S(1)}) custom-call(bf16[4,5,32,128]{3,2,1,0:T(8,128)(2,1)S(1)} %get-tuple-element.28.kept, bf16[4,5,32,128]{3,2,1,0:T(8,128)(2,1)S(1)} %collective-permute-done.5.received), custom_call_target="tpu_custom_call" | custom-call | tf_op jit(solution)/shard_map/fold/pallas_call | solution.py:45
  42.5 0.1 collective-permute-start.6
  42.6 5.5 %collective-permute-done.6.received = bf16[2,5,32,128]{3,2,1,0:T(8,128)(2,1)S(1)} collective-permute-done((bf16[2,5,32,128]{3,2,1,0:T(8,128)(2,1)S(1)}, bf16[2,5,32,128]{3,2,1,0:T(8,128)(2,1)S(1)}, u32[]{:S(2)}, u32[]{:S(2)}) %collective-permute-start.6) | collective-permute-done | bytes 81952 | tf_op jit(solution)/shard_map/ppermute | solution.py:389
  48.1 0.3 fold.3
  48.3 1.5 %collective-permute-start.7 = (bf16[1,5,32,128]{3,2,1,0:T(8,128)(2,1)S(1)}, bf16[1,5,32,128]{3,2,1,0:T(8,128)(2,1)S(1)}, u32[]{:S(2)}, u32[]{:S(2)}) collective-permute-start(bf16[1,5,32,128]{3,2,1,0:T(8,128)(2,1)S(1)} %get-tuple-element.33), channel_id=1, source_target_pairs={{0,8},{1,9},{2,10},{3,11},{4,12},{5,13},{6,14},{7,15},{8,0},{9,1},... | collective-permute-start | bytes 122888 | tf_op jit(solution)/shard_map/ppermute | solution.py:389
  49.9 2.4 %all-to-all-done.incoming = bf16[64,8,1024]{2,1,0:T(8,128)(2,1)S(1)} async-done(((bf16[64,8,1024]{2,1,0:T(8,128)(2,1)}), bf16[64,8,1024]{2,1,0:T(8,128)(2,1)S(1)}, u32[]{:S(2)}, u32[]{:S(2)}) %all-to-all-start) | async-done | bytes 1048608 | tf_op jit(solution)/shard_map/all_to_all | solution.py:448
  52.2 1.4 %settle.1 = bf16[32,8,1024]{2,1,0:T(8,128)(2,1)} custom-call(s32[8,128]{1,0:T(8,128)S(1)} %get-tuple-element.20.table_hbm.table, bf16[64,8,1024]{2,1,0:T(8,128)(2,1)S(1)} %all-to-all-done.incoming), custom_call_target="tpu_custom_call" | custom-call | tf_op jit(solution)/shard_map/settle/pallas_call | solution.py:45
  53.7 0.4 collective-permute-done.7.refs_1_
  54.1 0.8 %finish.1 = bf16[4,4096]{1,0:T(4,128)(2,1)} custom-call(bf16[1,5,32,128]{3,2,1,0:T(8,128)(2,1)S(1)} %get-tuple-element.36.refs_0_, bf16[1,5,32,128]{3,2,1,0:T(8,128)(2,1)S(1)} %collective-permute-done.7.refs_1_), custom_call_target="tpu_custom_call" | custom-call | tf_op jit(solution)/shard_map/finish/pallas_call | solution.py:45
Async XLA Ops:
  0.6 17.6 %collective-permute-start.1 = (bf16[4,4096]{1,0:T(4,128)(2,1)}, bf16[4,4096]{1,0:T(4,128)(2,1)S(1)}, u32[]{:S(2)}, u32[]{:S(2)}) collective-permute-start(bf16[4,4096]{1,0:T(4,128)(2,1)} %refs_0_.1), channel_id=1, source_target_pairs={{0,8},{1,9},{2,10},{3,11},{4,12},{5,13},{6,14},{7,15},{8,0},{9,1},... | collective-permute-start | bytes 98312 | tf_op jit(solution)/shard_map/ppermute | solution.py:389
  4.7 13.5 %collective-permute-start = (bf16[4,4096]{1,0:T(4,128)(2,1)}, bf16[4,4096]{1,0:T(4,128)(2,1)S(1)}, u32[]{:S(2)}, u32[]{:S(2)}) collective-permute-start(bf16[4,4096]{1,0:T(4,128)(2,1)} %refs_0_.1), channel_id=1, source_target_pairs={{0,4},{1,5},{2,6},{3,7},{4,0},{5,1},{6,2},{7,3},{8,12},{9,13},{10,... | collective-permute-start | bytes 98312 | tf_op jit(solution)/shard_map/ppermute | solution.py:389
  6.3 11.9 %collective-permute-start.2 = (bf16[4,4096]{1,0:T(4,128)(2,1)}, bf16[4,4096]{1,0:T(4,128)(2,1)S(1)}, u32[]{:S(2)}, u32[]{:S(2)}) collective-permute-start(bf16[4,4096]{1,0:T(4,128)(2,1)} %refs_0_.1), channel_id=1, source_target_pairs={{0,12},{1,13},{2,14},{3,15},{4,8},{5,9},{6,10},{7,11},{8,4},{9,5},... | collective-permute-start | bytes 98312 | tf_op jit(solution)/shard_map/ppermute | solution.py:389
  6.3 11.9 %copy-start = (bf16[4,4096]{1,0:T(4,128)(2,1)S(1)}, bf16[4,4096]{1,0:T(4,128)(2,1)}, u32[]{:S(2)}) copy-start(bf16[4,4096]{1,0:T(4,128)(2,1)} %refs_0_.1) | copy-start | bytes 98308
  19.9 8.8 %collective-permute-start.4 = (bf16[65,8,1024]{2,1,0:T(8,128)(2,1)S(1)}, bf16[65,8,1024]{2,1,0:T(8,128)(2,1)S(1)}, u32[]{:S(2)}, u32[]{:S(2)}) collective-permute-start(bf16[65,8,1024]{2,1,0:T(8,128)(2,1)S(1)} %get-tuple-element.26.pairs), channel_id=1, source_target_pairs={{0,1},{1,0},{2,3},{3,2},{4,5},{5,4},{6,7},{7,6},{8,9},{9,8},{10,11... | collective-permute-start | bytes 3194888 | tf_op jit(solution)/shard_map/ppermute | solution.py:389
  20.0 8.7 %collective-permute-start.3 = (bf16[4,4,32,128]{3,2,1,0:T(8,128)(2,1)S(1)}, bf16[4,4,32,128]{3,2,1,0:T(8,128)(2,1)S(1)}, u32[]{:S(2)}, u32[]{:S(2)}) collective-permute-start(bf16[4,4,32,128]{3,2,1,0:T(8,128)(2,1)S(1)} %get-tuple-element.25.queries), channel_id=1, source_target_pairs={{0,2},{1,3},{2,0},{3,1},{4,6},{5,7},{6,4},{7,5},{8,10},{9,11},{10,... | collective-permute-start | bytes 393224 | tf_op jit(solution)/shard_map/ppermute | solution.py:389
  21.8 30.5 %all-to-all-start = ((bf16[64,8,1024]{2,1,0:T(8,128)(2,1)}), bf16[64,8,1024]{2,1,0:T(8,128)(2,1)S(1)}, u32[]{:S(2)}, u32[]{:S(2)}) async-start(bf16[64,8,1024]{2,1,0:T(8,128)(2,1)} %get-tuple-element.34), calls=%async_computation | async-start | bytes 2097152 | tf_op jit(solution)/shard_map/all_to_all | solution.py:448
  31.6 10.3 %collective-permute-start.5 = (bf16[4,5,32,128]{3,2,1,0:T(8,128)(2,1)S(1)}, bf16[4,5,32,128]{3,2,1,0:T(8,128)(2,1)S(1)}, u32[]{:S(2)}, u32[]{:S(2)}) collective-permute-start(bf16[4,5,32,128]{3,2,1,0:T(8,128)(2,1)S(1)} %get-tuple-element.29), channel_id=1, source_target_pairs={{0,2},{1,3},{2,0},{3,1},{4,6},{5,7},{6,4},{7,5},{8,10},{9,11},{10,... | collective-permute-start | bytes 491528 | tf_op jit(solution)/shard_map/ppermute | solution.py:389
  42.5 5.6 %collective-permute-start.6 = (bf16[2,5,32,128]{3,2,1,0:T(8,128)(2,1)S(1)}, bf16[2,5,32,128]{3,2,1,0:T(8,128)(2,1)S(1)}, u32[]{:S(2)}, u32[]{:S(2)}) collective-permute-start(bf16[2,5,32,128]{3,2,1,0:T(8,128)(2,1)S(1)} %get-tuple-element.31), channel_id=1, source_target_pairs={{0,4},{1,5},{2,6},{3,7},{4,0},{5,1},{6,2},{7,3},{8,12},{9,13},{10,... | collective-permute-start | bytes 245768 | tf_op jit(solution)/shard_map/ppermute | solution.py:389
  48.3 5.8 %collective-permute-start.7 = (bf16[1,5,32,128]{3,2,1,0:T(8,128)(2,1)S(1)}, bf16[1,5,32,128]{3,2,1,0:T(8,128)(2,1)S(1)}, u32[]{:S(2)}, u32[]{:S(2)}) collective-permute-start(bf16[1,5,32,128]{3,2,1,0:T(8,128)(2,1)S(1)} %get-tuple-element.33), channel_id=1, source_target_pairs={{0,8},{1,9},{2,10},{3,11},{4,12},{5,13},{6,14},{7,15},{8,0},{9,1},... | collective-permute-start | bytes 122888 | tf_op jit(solution)/shard_map/ppermute | solution.py:389

commit v3 on v2

--- a/solution.py
+++ b/solution.py
@@ -55,7 +55,7 @@
 
 
 def split_sizes(width):
-    return tuple(width // 16 * units for units in (1, 2, 3, 3, 3, 2, 2))
+    return tuple(width // 16 * units for units in (1, 1, 2, 3, 3, 3, 2, 1))
 
 
 def iota(shape, axis):
@@ -75,8 +75,14 @@
         start = stop
 
 
+def seat(device, count):
+    back = count - 1 - device
+    return back ^ ((back < count // 2) * (count // 4))
+
+
 def places(device, holder, hist_ref, pack_ref, hold, owned, capacity):
     total = holder.shape[1]
+    count = hold // capacity
     local = holder - device * hold
     held = (local >= 0) & (local < hold)
     blocks = iota((hold, total), 1)
@@ -84,7 +90,7 @@
     block = lane_total(jnp.where(here, blocks, 0).astype(F32)).astype(I32)
     owner = block // owned
     rank = lane_total(jnp.where(held & (blocks < block) & (blocks >= owner * owned), 1.0, 0.0)).astype(I32)
-    target = jnp.clip(hold - (owner + 1) * capacity + jnp.minimum(rank, capacity - 1), 0, hold - 1)
+    target = jnp.minimum(seat(owner, count) * capacity + jnp.minimum(rank, capacity - 1), hold - 1)
     target = jnp.where(lane_total(jnp.where(here, 1.0, 0.0)) > 0, target, iota((hold, 1), 0))
     depth = jnp.zeros((hold, 1), I32)
     for _, start, stop in spans(hist_ref, pack_ref):
@@ -95,7 +101,7 @@
     keeper = holder // hold
     kept = lane_total(jnp.where(blocks == rows, keeper, 0).astype(F32)).astype(I32)
     order = lane_total(jnp.where((keeper == kept) & (blocks >= mine) & (blocks < rows), 1.0, 0.0)).astype(I32)
-    arrival = hold - (kept + 1) * capacity + jnp.minimum(order, capacity - 1)
+    arrival = seat(kept, count) * capacity + jnp.minimum(order, capacity - 1)
     arrival = jnp.concatenate([arrival, jnp.zeros((hold - owned, 1), I32)], axis=0)
     diagonal = iota((hold, HD), 0) == iota((hold, HD), 1)
     rows = [jnp.sum(jnp.where(diagonal, column, 0).astype(F32), axis=0, keepdims=True) for column in (target, arrival)]
@@ -148,6 +154,7 @@
 
     depart(0)
     depart(1)
+    depart(2)
 
     def multiply(part, lanes):
         offset, size, _, _ = copies[part]
@@ -158,7 +165,7 @@
     def arrive(part):
         for copy in copies[part][2:]:
             copy.wait()
-        depart(part + 2)
+        depart(part + 3)
 
     everything = slice(0, 2 * HALF)
     for part in range(2):
@@ -444,9 +451,9 @@
     outgoing, pairs, turned = lax.optimization_barrier((outgoing, pairs, turned))
     pairs_beside = swap(pairs, 1)
     turned_across = swap(turned, 2)
-    backwards = [list(range(count))[::-1]]
+    seats = [sorted(range(count), key=lambda member: seat(member, count))]
     incoming = lax.all_to_all(
-        outgoing, "req", split_axis=0, concat_axis=0, axis_index_groups=backwards, tiled=True
+        outgoing, "req", split_axis=0, concat_axis=0, axis_index_groups=seats, tiled=True
     )
     share = ((groups, KVH + 1, span, HD), BF16)
     keep, send = call(

time: 55.1 us -> 54 us (0.980)
  waiting for transfers between devices: 18 us -> 17 us
    ppermute x8, starting transfers between devices: 9.76 us -> 10.8 us  [swap(): return lax.ppermute(value, 'req', [(i, i ^ flip) for i in range(count)])]
    all_to_all x1, waiting for transfers between devices: 2.38 us -> 1.42 us  [on_device(): lax.all_to_all(outgoing, 'req', split_axis=0, concat_axis=0, axis_index_g...]
    all_to_all x1, starting transfers between devices: 6.89 us -> 6.11 us  [on_device(): lax.all_to_all(outgoing, 'req', split_axis=0, concat_axis=0, axis_index_g...]
where the time goes in v3:
time: 54 us; the launch traced here: 53.8 us
  Pallas kernels  19.2 us (36%)
  waiting for transfers between devices  17 us (31%)
  starting transfers between devices  16.9 us (31%)
  between operations  0.73 us (1%)
    pallas_call x7, Pallas kernels, call(): pl.pallas_call(kernel, out_shape=tuple((jax.ShapeDtypeStruct(shape, kind)...  19.2 us
    ppermute x8, waiting for transfers between devices, swap(): return lax.ppermute(value, 'req', [(i, i ^ flip) for i in range(count)])  15.6 us
    ppermute x8, starting transfers between devices, swap(): return lax.ppermute(value, 'req', [(i, i ^ flip) for i in range(count)])  10.8 us
    all_to_all x1, starting transfers between devices, on_device(): lax.all_to_all(outgoing, 'req', split_axis=0, concat_axis=0, axis_index_g...  6.11 us
    all_to_all x1, waiting for transfers between devices, on_device(): lax.all_to_all(outgoing, 'req', split_axis=0, concat_axis=0, axis_index_g...  1.42 us
  transfers between devices with their start and end apart: 9, of which 4 were waited for; matrix products, arithmetic and copies ran while one was open for 0% of the time, Pallas kernels for 31%

profile of v3, /device:TPU:0, one launch (start us, length us, event | category | flops | bytes accessed | tf_op | source)
XLA Modules:
  0.0 53.8 jit_solution(4211020172858929015)
XLA Ops:
  0.6 4.1 %collective-permute-start.1 = (bf16[4,4096]{1,0:T(4,128)(2,1)}, bf16[4,4096]{1,0:T(4,128)(2,1)S(1)}, u32[]{:S(2)}, u32[]{:S(2)}) collective-permute-start(bf16[4,4096]{1,0:T(4,128)(2,1)} %refs_0_.1), channel_id=1, source_target_pairs={{0,8},{1,9},{2,10},{3,11},{4,12},{5,13},{6,14},{7,15},{8,0},{9,1},... | collective-permute-start | bytes 98312 | tf_op jit(solution)/shard_map/ppermute | solution.py:396
  4.7 1.6 %collective-permute-start = (bf16[4,4096]{1,0:T(4,128)(2,1)}, bf16[4,4096]{1,0:T(4,128)(2,1)S(1)}, u32[]{:S(2)}, u32[]{:S(2)}) collective-permute-start(bf16[4,4096]{1,0:T(4,128)(2,1)} %refs_0_.1), channel_id=1, source_target_pairs={{0,4},{1,5},{2,6},{3,7},{4,0},{5,1},{6,2},{7,3},{8,12},{9,13},{10,... | collective-permute-start | bytes 98312 | tf_op jit(solution)/shard_map/ppermute | solution.py:396
  6.3 0.0 collective-permute-start.2
  6.3 0.0 copy-start
  6.3 11.5 %project.1 = (bf16[65,8,1024]{2,1,0:T(8,128)(2,1)S(1)}, s32[8,128]{1,0:T(8,128)S(1)}, f32[20,512]{1,0:T(8,128)S(1)}, f32[4,2,8,128]{3,2,1,0:T(8,128)S(1)}) custom-call(s32[4]{0:T(128)} %hist_hbm.1, s32[4]{0:T(128)} %pack_hbm.1, s32[4]{0:T(128)} %len_hbm.1, s32[1,512]{1,0:T(1,128)} %bitcast.1, f32[1,128]{1,0:T(1,128)} %constant.2.clone.wave_hbm, ...), custom_call_target="tpu_custom_call" | custom-call | tf_op jit(solution)/shard_map/project/pallas_call | solution.py:45
  17.9 0.0 collective-permute-done.1.refs_2_
  17.9 0.0 collective-permute-done.refs_1_
  17.9 0.0 collective-permute-done.2.refs_3_
  17.9 0.0 copy-done
  17.9 1.6 %ship.1 = (bf16[64,8,1024]{2,1,0:T(8,128)(2,1)}, bf16[4,4,32,128]{3,2,1,0:T(8,128)(2,1)S(1)}) custom-call(s32[8,128]{1,0:T(8,128)S(1)} %get-tuple-element.20.table_hbm.table, bf16[65,8,1024]{2,1,0:T(8,128)(2,1)S(1)} %get-tuple-element.26.pairs, f32[4,2,8,128]{3,2,1,0:T(8,128)S(1)} %get-tuple-element.22.turns, bf16[4,4096]{1,0:T(4,128)(2,1)S(1)} %copy-done, ...), custom_call_target="tpu_custom_call" | custom-call | tf_op jit(solution)/shard_map/ship/pallas_call | solution.py:45
  19.5 0.1 collective-permute-start.4
  19.6 1.8 %collective-permute-start.3 = (bf16[4,4,32,128]{3,2,1,0:T(8,128)(2,1)S(1)}, bf16[4,4,32,128]{3,2,1,0:T(8,128)(2,1)S(1)}, u32[]{:S(2)}, u32[]{:S(2)}) collective-permute-start(bf16[4,4,32,128]{3,2,1,0:T(8,128)(2,1)S(1)} %get-tuple-element.25.queries), channel_id=1, source_target_pairs={{0,2},{1,3},{2,0},{3,1},{4,6},{5,7},{6,4},{7,5},{8,10},{9,11},{10,... | collective-permute-start | bytes 393224 | tf_op jit(solution)/shard_map/ppermute | solution.py:396
  21.4 6.1 %all-to-all-start = ((bf16[64,8,1024]{2,1,0:T(8,128)(2,1)}), bf16[64,8,1024]{2,1,0:T(8,128)(2,1)S(1)}, u32[]{:S(2)}, u32[]{:S(2)}) async-start(bf16[64,8,1024]{2,1,0:T(8,128)(2,1)} %get-tuple-element.34), calls=%async_computation | async-start | bytes 2097152 | tf_op jit(solution)/shard_map/all_to_all | solution.py:455
  27.5 0.0 collective-permute-done.3.queries_across
  27.5 0.0 collective-permute-done.4.pairs_beside
  27.5 2.9 %attend.1 = (bf16[4,5,32,128]{3,2,1,0:T(8,128)(2,1)S(1)}, bf16[4,5,32,128]{3,2,1,0:T(8,128)(2,1)S(1)}) custom-call(bf16[4,4,32,128]{3,2,1,0:T(8,128)(2,1)S(1)} %get-tuple-element.25.queries, bf16[4,4,32,128]{3,2,1,0:T(8,128)(2,1)S(1)} %collective-permute-done.3.queries_across, bf16[65,8,1024]{2,1,0:T(8,128)(2,1)S(1)} %get-tuple-element.26.pairs, ...), custom_call_target="tpu_custom_call" | custom-call | flops 60000002048 | tf_op jit(solution)/shard_map/attend/pallas_call | solution.py:45
  30.5 0.6 %collective-permute-start.5 = (bf16[4,5,32,128]{3,2,1,0:T(8,128)(2,1)S(1)}, bf16[4,5,32,128]{3,2,1,0:T(8,128)(2,1)S(1)}, u32[]{:S(2)}, u32[]{:S(2)}) collective-permute-start(bf16[4,5,32,128]{3,2,1,0:T(8,128)(2,1)S(1)} %get-tuple-element.29), channel_id=1, source_target_pairs={{0,2},{1,3},{2,0},{3,1},{4,6},{5,7},{6,4},{7,5},{8,10},{9,11},{10,... | collective-permute-start | bytes 491528 | tf_op jit(solution)/shard_map/ppermute | solution.py:396
  31.1 9.9 %collective-permute-done.5.received = bf16[4,5,32,128]{3,2,1,0:T(8,128)(2,1)S(1)} collective-permute-done((bf16[4,5,32,128]{3,2,1,0:T(8,128)(2,1)S(1)}, bf16[4,5,32,128]{3,2,1,0:T(8,128)(2,1)S(1)}, u32[]{:S(2)}, u32[]{:S(2)}) %collective-permute-start.5) | collective-permute-done | bytes 163872 | tf_op jit(solution)/shard_map/ppermute | solution.py:396
  41.0 0.6 %fold.2 = (bf16[2,5,32,128]{3,2,1,0:T(8,128)(2,1)S(1)}, bf16[2,5,32,128]{3,2,1,0:T(8,128)(2,1)S(1)}) custom-call(bf16[4,5,32,128]{3,2,1,0:T(8,128)(2,1)S(1)} %get-tuple-element.28.kept, bf16[4,5,32,128]{3,2,1,0:T(8,128)(2,1)S(1)} %collective-permute-done.5.received), custom_call_target="tpu_custom_call" | custom-call | tf_op jit(solution)/shard_map/fold/pallas_call | solution.py:45
  41.6 0.1 collective-permute-start.6
  41.7 5.2 %collective-permute-done.6.received = bf16[2,5,32,128]{3,2,1,0:T(8,128)(2,1)S(1)} collective-permute-done((bf16[2,5,32,128]{3,2,1,0:T(8,128)(2,1)S(1)}, bf16[2,5,32,128]{3,2,1,0:T(8,128)(2,1)S(1)}, u32[]{:S(2)}, u32[]{:S(2)}) %collective-permute-start.6) | collective-permute-done | bytes 81952 | tf_op jit(solution)/shard_map/ppermute | solution.py:396
  46.9 0.3 fold.3
  47.2 2.5 %collective-permute-start.7 = (bf16[1,5,32,128]{3,2,1,0:T(8,128)(2,1)S(1)}, bf16[1,5,32,128]{3,2,1,0:T(8,128)(2,1)S(1)}, u32[]{:S(2)}, u32[]{:S(2)}) collective-permute-start(bf16[1,5,32,128]{3,2,1,0:T(8,128)(2,1)S(1)} %get-tuple-element.33), channel_id=1, source_target_pairs={{0,8},{1,9},{2,10},{3,11},{4,12},{5,13},{6,14},{7,15},{8,0},{9,1},... | collective-permute-start | bytes 122888 | tf_op jit(solution)/shard_map/ppermute | solution.py:396
  49.7 1.4 %all-to-all-done.incoming = bf16[64,8,1024]{2,1,0:T(8,128)(2,1)S(1)} async-done(((bf16[64,8,1024]{2,1,0:T(8,128)(2,1)}), bf16[64,8,1024]{2,1,0:T(8,128)(2,1)S(1)}, u32[]{:S(2)}, u32[]{:S(2)}) %all-to-all-start) | async-done | bytes 1048608 | tf_op jit(solution)/shard_map/all_to_all | solution.py:455
  51.1 1.4 %settle.1 = bf16[32,8,1024]{2,1,0:T(8,128)(2,1)} custom-call(s32[8,128]{1,0:T(8,128)S(1)} %get-tuple-element.20.table_hbm.table, bf16[64,8,1024]{2,1,0:T(8,128)(2,1)S(1)} %all-to-all-done.incoming), custom_call_target="tpu_custom_call" | custom-call | tf_op jit(solution)/shard_map/settle/pallas_call | solution.py:45
  52.6 0.4 collective-permute-done.7.refs_1_
  53.0 0.8 %finish.1 = bf16[4,4096]{1,0:T(4,128)(2,1)} custom-call(bf16[1,5,32,128]{3,2,1,0:T(8,128)(2,1)S(1)} %get-tuple-element.36.refs_0_, bf16[1,5,32,128]{3,2,1,0:T(8,128)(2,1)S(1)} %collective-permute-done.7.refs_1_), custom_call_target="tpu_custom_call" | custom-call | tf_op jit(solution)/shard_map/finish/pallas_call | solution.py:45
Async XLA Ops:
  0.6 17.2 %collective-permute-start.1 = (bf16[4,4096]{1,0:T(4,128)(2,1)}, bf16[4,4096]{1,0:T(4,128)(2,1)S(1)}, u32[]{:S(2)}, u32[]{:S(2)}) collective-permute-start(bf16[4,4096]{1,0:T(4,128)(2,1)} %refs_0_.1), channel_id=1, source_target_pairs={{0,8},{1,9},{2,10},{3,11},{4,12},{5,13},{6,14},{7,15},{8,0},{9,1},... | collective-permute-start | bytes 98312 | tf_op jit(solution)/shard_map/ppermute | solution.py:396
  4.7 13.1 %collective-permute-start = (bf16[4,4096]{1,0:T(4,128)(2,1)}, bf16[4,4096]{1,0:T(4,128)(2,1)S(1)}, u32[]{:S(2)}, u32[]{:S(2)}) collective-permute-start(bf16[4,4096]{1,0:T(4,128)(2,1)} %refs_0_.1), channel_id=1, source_target_pairs={{0,4},{1,5},{2,6},{3,7},{4,0},{5,1},{6,2},{7,3},{8,12},{9,13},{10,... | collective-permute-start | bytes 98312 | tf_op jit(solution)/shard_map/ppermute | solution.py:396
  6.3 11.6 %collective-permute-start.2 = (bf16[4,4096]{1,0:T(4,128)(2,1)}, bf16[4,4096]{1,0:T(4,128)(2,1)S(1)}, u32[]{:S(2)}, u32[]{:S(2)}) collective-permute-start(bf16[4,4096]{1,0:T(4,128)(2,1)} %refs_0_.1), channel_id=1, source_target_pairs={{0,12},{1,13},{2,14},{3,15},{4,8},{5,9},{6,10},{7,11},{8,4},{9,5},... | collective-permute-start | bytes 98312 | tf_op jit(solution)/shard_map/ppermute | solution.py:396
  6.3 11.6 %copy-start = (bf16[4,4096]{1,0:T(4,128)(2,1)S(1)}, bf16[4,4096]{1,0:T(4,128)(2,1)}, u32[]{:S(2)}) copy-start(bf16[4,4096]{1,0:T(4,128)(2,1)} %refs_0_.1) | copy-start | bytes 98308
  19.5 8.0 %collective-permute-start.4 = (bf16[65,8,1024]{2,1,0:T(8,128)(2,1)S(1)}, bf16[65,8,1024]{2,1,0:T(8,128)(2,1)S(1)}, u32[]{:S(2)}, u32[]{:S(2)}) collective-permute-start(bf16[65,8,1024]{2,1,0:T(8,128)(2,1)S(1)} %get-tuple-element.26.pairs), channel_id=1, source_target_pairs={{0,1},{1,0},{2,3},{3,2},{4,5},{5,4},{6,7},{7,6},{8,9},{9,8},{10,11... | collective-permute-start | bytes 3194888 | tf_op jit(solution)/shard_map/ppermute | solution.py:396
  19.6 7.9 %collective-permute-start.3 = (bf16[4,4,32,128]{3,2,1,0:T(8,128)(2,1)S(1)}, bf16[4,4,32,128]{3,2,1,0:T(8,128)(2,1)S(1)}, u32[]{:S(2)}, u32[]{:S(2)}) collective-permute-start(bf16[4,4,32,128]{3,2,1,0:T(8,128)(2,1)S(1)} %get-tuple-element.25.queries), channel_id=1, source_target_pairs={{0,2},{1,3},{2,0},{3,1},{4,6},{5,7},{6,4},{7,5},{8,10},{9,11},{10,... | collective-permute-start | bytes 393224 | tf_op jit(solution)/shard_map/ppermute | solution.py:396
  21.4 29.7 %all-to-all-start = ((bf16[64,8,1024]{2,1,0:T(8,128)(2,1)}), bf16[64,8,1024]{2,1,0:T(8,128)(2,1)S(1)}, u32[]{:S(2)}, u32[]{:S(2)}) async-start(bf16[64,8,1024]{2,1,0:T(8,128)(2,1)} %get-tuple-element.34), calls=%async_computation | async-start | bytes 2097152 | tf_op jit(solution)/shard_map/all_to_all | solution.py:455
  30.5 10.5 %collective-permute-start.5 = (bf16[4,5,32,128]{3,2,1,0:T(8,128)(2,1)S(1)}, bf16[4,5,32,128]{3,2,1,0:T(8,128)(2,1)S(1)}, u32[]{:S(2)}, u32[]{:S(2)}) collective-permute-start(bf16[4,5,32,128]{3,2,1,0:T(8,128)(2,1)S(1)} %get-tuple-element.29), channel_id=1, source_target_pairs={{0,2},{1,3},{2,0},{3,1},{4,6},{5,7},{6,4},{7,5},{8,10},{9,11},{10,... | collective-permute-start | bytes 491528 | tf_op jit(solution)/shard_map/ppermute | solution.py:396
  41.6 5.3 %collective-permute-start.6 = (bf16[2,5,32,128]{3,2,1,0:T(8,128)(2,1)S(1)}, bf16[2,5,32,128]{3,2,1,0:T(8,128)(2,1)S(1)}, u32[]{:S(2)}, u32[]{:S(2)}) collective-permute-start(bf16[2,5,32,128]{3,2,1,0:T(8,128)(2,1)S(1)} %get-tuple-element.31), channel_id=1, source_target_pairs={{0,4},{1,5},{2,6},{3,7},{4,0},{5,1},{6,2},{7,3},{8,12},{9,13},{10,... | collective-permute-start | bytes 245768 | tf_op jit(solution)/shard_map/ppermute | solution.py:396
  47.2 5.8 %collective-permute-start.7 = (bf16[1,5,32,128]{3,2,1,0:T(8,128)(2,1)S(1)}, bf16[1,5,32,128]{3,2,1,0:T(8,128)(2,1)S(1)}, u32[]{:S(2)}, u32[]{:S(2)}) collective-permute-start(bf16[1,5,32,128]{3,2,1,0:T(8,128)(2,1)S(1)} %get-tuple-element.33), channel_id=1, source_target_pairs={{0,8},{1,9},{2,10},{3,11},{4,12},{5,13},{6,14},{7,15},{8,0},{9,1},... | collective-permute-start | bytes 122888 | tf_op jit(solution)/shard_map/ppermute | solution.py:396
